TPU v7x, 128 devices: a whole 4x4x4 slice. The times are simulated.
128 devices in a mesh: dp: 32 (over z, x, y_lo), expert: 4 (over y_hi, core).
Axes of the slice: x: 4, y: 4 (y_hi: 2, y_lo: 2; y = y_hi * 2 + y_lo), z: 4, core: 2. Of those that a mesh axis runs over, the one named last changes fastest.
Arguments:
- tokens: bfloat16 [65536, 2048], P(('dp', 'expert')), may hold values from -6 to 6
- out_grad: bfloat16 [65536, 2048], P(('dp', 'expert')), may hold values from -6 to 6
- chosen: int32 [4, 1024], replicated, may hold values from 0 to 65535, as said below
- slot_weight: float32 [4, 1024], P('expert'), may hold values from 0.05 to 1
- w_gate: bfloat16 [4, 2048, 1408], P('expert'), may hold values from -0.125 to 0.125
- w_up: bfloat16 [4, 2048, 1408], P('expert'), may hold values from -0.125 to 0.125
- w_down: bfloat16 [4, 1408, 2048], P('expert'), may hold values from -0.15625 to 0.15625
Outputs:
- token_grad: bfloat16 [65536, 2048], P(('dp', 'expert'))
- grad_gate: bfloat16 [4, 2048, 1408], P('expert', 'dp')
- grad_up: bfloat16 [4, 2048, 1408], P('expert', 'dp')
- grad_down: bfloat16 [4, 1408, 2048], P('expert', 'dp')
Inputs may be any that keep to these rules, and one draw needn't show every extreme that they name: `chosen`: the tokens of device q, counted with dp before expert, are positions q * 512 to (q + 1) * 512 - 1; token group g is the 4 devices with dp index g. The entries of one expert's list are distinct; at most 16 of them lie on one device, and in every list there is a token group each of whose devices holds exactly 16 of them.
All inputs are finite; a program needn't handle non-finite values.
Results may differ from a plain program's by a relative error of at most 0.03.
Values may be sent and summed in bfloat16 or wider, within the bound.
A program may use at most 192 MiB of HBM per device.

v0:
```python
import jax
import jax.numpy as jnp
from jax import lax
from jax.sharding import PartitionSpec as P

MOST = 16


def rank_slots(live, limit):
    running = jnp.cumsum(live.astype(jnp.int32), axis=1)
    wanted = jnp.arange(limit, dtype=jnp.int32)
    picked = jnp.sum((running[:, None, :] < (wanted + 1)[None, :, None]).astype(jnp.int32), axis=2)
    present = wanted[None, :] < running[:, -1:]
    return (jnp.minimum(picked, live.shape[1] - 1), present)


def contract_rows(left_rows, right_rows):
    return lax.dot_general(
        left_rows, right_rows, (((0,), (0,)), ((), ())), preferred_element_type=jnp.float32
    )


def local(tokens, out_grad, chosen, slot_weight, w_gate, w_up, w_down):
    expert_id = lax.axis_index("expert")
    group_id = lax.axis_index("dp")
    groups = lax.axis_size("expert")
    replicas = lax.axis_size("dp")
    tok_dev, width = tokens.shape
    group_rows = tok_dev * groups
    my_list = lax.dynamic_index_in_dim(chosen, expert_id, 0, keepdims=False)
    in_group = my_list // group_rows == group_id
    owner_of = my_list % group_rows // tok_dev
    member = in_group[None, :] & (owner_of[None, :] == jnp.arange(groups, dtype=jnp.int32)[:, None])
    slot_pick, slot_present = rank_slots(member, MOST)
    weights = jnp.where(slot_present, slot_weight[0][slot_pick], 0.0).reshape(-1)
    gate_matrix = w_gate[0]
    up_matrix = w_up[0]
    down_matrix = w_down[0]
    zero_value = jnp.zeros((), tokens.dtype)
    device_id = group_id * groups + expert_id
    owned_slots = chosen // tok_dev == device_id
    out_pick, out_present = rank_slots(owned_slots, MOST)
    local_rows = jnp.take_along_axis(chosen, out_pick, axis=1) % tok_dev
    send_tokens = jnp.where(out_present[..., None], tokens[local_rows], zero_value)
    send_grads = jnp.where(out_present[..., None], out_grad[local_rows], zero_value)
    got_tokens, got_grads = (
        lax.all_to_all(send_tokens, "expert", split_axis=0, concat_axis=0, tiled=True),
        lax.all_to_all(send_grads, "expert", split_axis=0, concat_axis=0, tiled=True),
    )
    chosen_rows = got_tokens.reshape(-1, width)
    chosen_grads = got_grads.reshape(-1, width)
    gate_pre = jnp.dot(chosen_rows, gate_matrix, preferred_element_type=jnp.float32)
    up_pre = jnp.dot(chosen_rows, up_matrix, preferred_element_type=jnp.float32)
    sigmoid_gate = 1.0 / (1.0 + jnp.exp(-gate_pre))
    activated = gate_pre * sigmoid_gate
    hidden = (activated * up_pre).astype(jnp.bfloat16)
    grad_out = (weights[:, None] * chosen_grads.astype(jnp.float32)).astype(jnp.bfloat16)
    grad_hidden = lax.dot_general(
        grad_out, down_matrix, (((1,), (1,)), ((), ())), preferred_element_type=jnp.float32
    )
    grad_gate_pre = (
        grad_hidden * up_pre * (sigmoid_gate * (1.0 + gate_pre * (1.0 - sigmoid_gate)))
    ).astype(jnp.bfloat16)
    grad_up_pre = (grad_hidden * activated).astype(jnp.bfloat16)
    part_gate = contract_rows(chosen_rows, grad_gate_pre)
    part_up = contract_rows(chosen_rows, grad_up_pre)
    part_down = contract_rows(hidden, grad_out)
    total_gate, total_up, total_down = (
        lax.psum_scatter(
            part_gate.astype(jnp.bfloat16), "dp", scatter_dimension=0, tiled=True
        ).astype(jnp.float32),
        lax.psum_scatter(
            part_up.astype(jnp.bfloat16), "dp", scatter_dimension=0, tiled=True
        ).astype(jnp.float32),
        lax.psum_scatter(
            part_down.astype(jnp.bfloat16), "dp", scatter_dimension=0, tiled=True
        ).astype(jnp.float32),
    )
    slot_grad = lax.dot_general(
        grad_gate_pre, gate_matrix, (((1,), (1,)), ((), ())), preferred_element_type=jnp.float32
    ) + lax.dot_general(
        grad_up_pre, up_matrix, (((1,), (1,)), ((), ())), preferred_element_type=jnp.float32
    )
    slot_grad = jnp.where(slot_present.reshape(-1)[:, None], slot_grad, 0.0)
    send_back = slot_grad.reshape(groups, MOST, width)
    got_back = lax.all_to_all(
        send_back.astype(jnp.bfloat16), "expert", split_axis=0, concat_axis=0, tiled=True
    ).astype(send_back.dtype)
    kept_back = jnp.where(out_present[..., None], got_back, 0.0)
    token_sum = (
        jnp.zeros((tok_dev, width), jnp.float32)
        .at[local_rows.reshape(-1)]
        .add(kept_back.reshape(-1, width))
    )
    grad_scale = 1.0 / replicas
    return (
        token_sum.astype(jnp.bfloat16),
        (total_gate * grad_scale).astype(jnp.bfloat16)[None],
        (total_up * grad_scale).astype(jnp.bfloat16)[None],
        (total_down * grad_scale).astype(jnp.bfloat16)[None],
    )


def solution(mesh):
    return jax.shard_map(
        local,
        mesh=mesh,
        in_specs=(
            P(("dp", "expert"), None),
            P(("dp", "expert"), None),
            P(),
            P("expert", None),
            P("expert", None, None),
            P("expert", None, None),
            P("expert", None, None),
        ),
        out_specs=(
            P(("dp", "expert"), None),
            P("expert", "dp", None),
            P("expert", "dp", None),
            P("expert", "dp", None),
        ),
        check_vma=False,
    )
```

profile of v0, /device:TPU:0, one launch (start us, length us, event | category | flops | bytes accessed | tf_op | source)
XLA Modules:
  0.0 492.6 jit_solution(18000048624172202222)
XLA Ops:
  7.2 0.0 copy-start
  7.2 0.9 compare_reduce_fusion
  8.2 1.1 reduce-window.16
  9.3 0.2 slice_reduce_fusion
  9.5 0.2 reduce-window.19
  9.7 0.1 add_bitcast_fusion
  9.8 0.8 convert_bitcast_fusion
  10.6 1.1 reduce-window.14
  11.7 0.2 slice_reduce_fusion.1
  11.9 0.2 reduce-window.15
  12.1 0.1 add_bitcast_fusion.1
  12.2 0.1 slice.36
  12.3 0.3 convert_reduce_fusion
  12.6 0.1 reshape.357
  12.7 1.6 gather_fusion.3
  14.3 0.1 gather.22
  14.4 0.1 reshape.343
  14.5 0.7 gather_fusion.2
  15.3 2.9 gather_fusion.1
  18.1 0.1 copy.19
  18.2 0.1 iota_compare_fusion.2
  18.3 0.9 broadcast_select_fusion.1
  19.2 4.5 all-to-all-start.1
  23.7 0.1 slice.38
  23.8 0.1 reshape.335
  23.9 0.1 copy.20
  24.0 0.7 gather_fusion
  24.7 0.1 reshape.334
  24.8 0.1 broadcast_select_fusion.2
  24.9 6.4 %all-to-all-done.1 = bf16[4,16,2048]{2,1,0:T(8,128)(2,1)S(1)} async-done(((bf16[4,16,2048]{2,1,0:T(8,128)(2,1)}), bf16[4,16,2048]{2,1,0:T(8,128)(2,1)S(1)}, u32[]{:S(2)}, u32[]{:S(2)}) %all-to-all-start.1) | async-done | bytes 262176 | tf_op jit(solution)/shard_map/all_to_all | solution.py:47
  31.3 3.4 all-to-all-start
  34.7 0.0 reduce-scatter.5.cloned.1.call-start
  34.7 3.7 fusion.3
  38.4 3.7 fusion.7
  42.2 0.0 all-to-all-done
  42.2 0.1 multiply_convert_fusion
  42.3 4.5 multiply_convert_fusion.5
  46.8 0.7 copy-done.2
  47.5 4.2 convolution_convert_fusion.2
  51.7 0.0 reduce-scatter.5.cloned.1.call-update
  51.7 0.0 reduce-scatter.7.cloned.1.call-start
  51.8 4.3 convolution_convert_fusion.1
  56.0 0.0 reduce-scatter.7.cloned.1.call-update
  56.1 0.1 iota_compare_fusion.1
  56.1 0.1 lt.170
  56.2 0.1 min.44
  56.3 0.6 dynamic-slice.4
  57.6 4.5 fusion.1
  62.1 5.4 %fusion.17 = bf16[64,2048]{1,0:T(8,128)(2,1)} fusion(f32[64,2048]{1,0:T(8,128)S(1)} %fusion.1, bf16[64,1408]{1,0:T(8,128)(2,1)S(1)} %get-tuple-element.8, bf16[1,2048,1408]{2,1,0:T(8,128)(2,1)} %param.12, pred[64]{0:T(512)(128)(4,1)S(1)} %lt.170), kind=kOutput, calls=%fused_computation.20 | convolution fusion | flops 369491968 | bytes 6733888 | tf_op jit(solution)/shard_map/dot_general | solution.py:81
  67.4 4.7 all-to-all-start.2
  72.1 0.1 fusion.22
  72.2 4.2 convolution_convert_fusion
  76.4 256.2 %fusion = bf16[48,2048]{1,0:T(8,128)(2,1)S(1)} fusion(bf16[1408,2048]{1,0:T(8,128)(2,1)} %convolution_convert_fusion), kind=kCustom, calls=%all-reduce-scatter | all-reduce-scatter fusion | flops 3145729 | bytes 5964288
  332.6 3.3 collective-permute-start
  336.0 1.7 collective-permute-start.1
  337.6 3.8 collective-permute-start.2
  341.4 1.1 convert_select_fusion
  342.5 3.6 scatter_custom_fusion
  346.1 3.8 convert_element_type.87
  350.0 1.0 concatenate.3
  350.9 0.7 fusion.24
  351.7 1.6 fusion.25
  353.3 130.8 %reduce-scatter.7.cloned.1.call-done = bf16[64,1408]{1,0:T(8,128)(2,1)} async-done(((bf16[2048,1408]{1,0:T(8,128)(2,1)}), bf16[64,1408]{1,0:T(8,128)(2,1)}) %reduce-scatter.7.cloned.1.call-update) | async-done | bytes 180240 | tf_op jit(solution)/shard_map/reduce_scatter | solution.py:72
  484.1 1.6 fusion.26
  (27 shorter events, 0.2 us)
Async XLA Ops:
  7.2 7.3 %copy-start = (bf16[512,2048]{1,0:T(8,128)(2,1)S(1)}, bf16[512,2048]{1,0:T(8,128)(2,1)}, u32[]{:S(2)}) copy-start(bf16[512,2048]{1,0:T(8,128)(2,1)} %param.7) | copy-start | bytes 6291460
  7.2 16.8 %copy-start.1 = (f32[1,1024]{1,0:T(1,128)S(1)}, f32[1,1024]{1,0:T(1,128)}, u32[]{:S(2)}) copy-start(f32[1,1024]{1,0:T(1,128)} %param.10) | copy-start | bytes 12292
  19.2 12.1 %all-to-all-start.1 = ((bf16[4,16,2048]{2,1,0:T(8,128)(2,1)}), bf16[4,16,2048]{2,1,0:T(8,128)(2,1)S(1)}, u32[]{:S(2)}, u32[]{:S(2)}) async-start(bf16[4,16,2048]{2,1,0:T(8,128)(2,1)} %get-tuple-element.11), calls=%async_computation.1 | async-start | bytes 524288 | tf_op jit(solution)/shard_map/all_to_all | solution.py:47
  31.3 10.9 %all-to-all-start = ((bf16[4,16,2048]{2,1,0:T(8,128)(2,1)}), bf16[4,16,2048]{2,1,0:T(8,128)(2,1)S(1)}, u32[]{:S(2)}, u32[]{:S(2)}) async-start(bf16[4,16,2048]{2,1,0:T(8,128)(2,1)} %get-tuple-element.10), calls=%async_computation | async-start | bytes 524288 | tf_op jit(solution)/shard_map/all_to_all | solution.py:48
  34.7 317.0 %reduce-scatter.5.cloned.1.call-start = ((), (), s32[]{:S(2)}) async-start(), calls=%async_computation.5 | async-start | bytes 5947392 | tf_op jit(solution)/shard_map/reduce_scatter | solution.py:69
  46.8 0.7 copy-start.2
  51.7 432.4 %reduce-scatter.7.cloned.1.call-start = ((), (), s32[]{:S(2)}) async-start(), calls=%async_computation.6 | async-start | bytes 5947392 | tf_op jit(solution)/shard_map/reduce_scatter | solution.py:72
  51.8 4.6 copy-start.4
  56.0 1.6 copy-start.3
  67.4 274.0 %all-to-all-start.2 = ((bf16[4,16,2048]{2,1,0:T(8,128)(2,1)}), bf16[4,16,2048]{2,1,0:T(8,128)(2,1)}, u32[]{:S(2)}, u32[]{:S(2)}) async-start(bf16[4,16,2048]{2,1,0:T(8,128)(2,1)} %bitcast.15), calls=%async_computation.2 | async-start | bytes 524288 | tf_op jit(solution)/shard_map/all_to_all | solution.py:86
  332.6 17.3 %collective-permute-start = (bf16[48,2048]{1,0:T(8,128)(2,1)S(1)}, bf16[48,2048]{1,0:T(8,128)(2,1)S(1)}, u32[]{:S(2)}, u32[]{:S(2)}) collective-permute-start(bf16[48,2048]{1,0:T(8,128)(2,1)S(1)} %fusion), channel_id=1, source_target_pairs={{0,4},{4,8},{8,12},{12,16},{16,20},{20,24},{24,28},{28,32},{32,36}... | collective-permute-start | bytes 589832
  336.0 14.0 %collective-permute-start.1 = (bf16[48,2048]{1,0:T(8,128)(2,1)S(1)}, bf16[48,2048]{1,0:T(8,128)(2,1)S(1)}, u32[]{:S(2)}, u32[]{:S(2)}) collective-permute-start(bf16[48,2048]{1,0:T(8,128)(2,1)S(1)} %fusion), channel_id=1, source_target_pairs={{0,8},{4,12},{8,16},{12,20},{16,24},{20,28},{24,32},{28,36},{32,40... | collective-permute-start | bytes 589832
  337.6 12.3 %collective-permute-start.2 = (bf16[28,2048]{1,0:T(8,128)(2,1)S(1)}, bf16[28,2048]{1,0:T(8,128)(2,1)S(1)}, u32[]{:S(2)}, u32[]{:S(2)}) collective-permute-start(bf16[28,2048]{1,0:T(8,128)(2,1)S(1)} %slice.39), channel_id=1, source_target_pairs={{0,12},{4,16},{8,20},{12,24},{16,28},{20,32},{24,36},{28,40},{32,4... | collective-permute-start | bytes 344072
Sparse Core Ops, SparseCore 0:
  51.8 248.3 reduce-scatter.4
  302.6 181.4 reduce-scatter.6
where the time goes:
time: 494 us; the launch traced here: 493 us
  blocking collectives  256 us (52%)
  waiting for transfers between devices  137 us (28%)
  matrix products  34.4 us (7%)
  starting transfers between devices  21.5 us (4%)
  other arithmetic  18.7 us (4%)
  between operations  14.9 us (3%)
  local copies, waits for them, and re-layouts  9.59 us (2%)
    unnamed x1, blocking collectives  256 us
    reduce_scatter x1, waiting for transfers between devices, local(): lax.psum_scatter(part_up.astype(jnp.bfloat16), 'dp', scatter_dimension=0,...  131 us
    dot_general x3, matrix products, contract_rows(): lax.dot_general(left_rows, right_rows, (((0,), (0,)), ((), ())), preferre...  12.6 us
  transfers between devices with their start and end apart: 8, of which 2 were waited for; matrix products, arithmetic and copies ran while one was open for 60% of the time, Pallas kernels for 0%

commit v1 on v0

v1 whole, which is shorter than its diff:
```python
import functools

import jax
import jax.numpy as jnp
from jax import lax
from jax.experimental import pallas as pl
from jax.experimental.pallas import tpu as pltpu
from jax.sharding import PartitionSpec as P

MESH = pl.DeviceIdType.MESH
BF = jnp.bfloat16
F32 = jnp.float32
MOST = 16
SLOTS = 64
QUARTER = 352
QPAD = 384
NN = (((1,), (0,)), ((), ()))
NT = (((1,), (1,)), ((), ()))
TN = (((0,), (0,)), ((), ()))


def dot(lhs, rhs, dims):
    return lax.dot_general(lhs, rhs, dims, preferred_element_type=F32)


def indicator(cond):
    return jnp.where(cond, 1.0, 0.0).astype(BF)


def route_kernel(chosen, slot_weight, tokens, out_grad, rows_out, grads_out, pick_out, weight_out,
                 tok_buf, grad_buf, sems):
    loads = [
        pltpu.make_async_copy(tokens, tok_buf, sems.at[0]),
        pltpu.make_async_copy(out_grad, grad_buf, sems.at[1]),
    ]
    for load in loads:
        load.start()
    dp = lax.axis_index("dp")
    me = lax.axis_index("expert")
    slots = chosen.shape[1]
    row = lax.broadcasted_iota(jnp.int32, (16, slots), 0)
    low_iota = lax.broadcasted_iota(jnp.int32, (128, slots), 0)
    counts = jnp.zeros((16, 128), F32)
    for n in range(4):
        entries = chosen[pl.ds((me + n) % 4, 1), :]
        high = (entries >> 7) - (dp * 4 + me) * 4
        high = jnp.where((high >= 0) & (high < 4), high + 4 * n, -1)
        counts = counts + dot(indicator(row == high), indicator(low_iota == (entries & 127)), NT)
    entries = chosen[pl.ds(me, 1), :]
    high = (entries >> 7) - dp * 16
    wanted = 4 * ((me + 4 - (row >> 2)) & 3) + (row & 3)
    hit = wanted == high
    low = indicator(low_iota == (entries & 127))
    group_counts = dot(indicator(hit), low, NT)
    value = slot_weight[...]
    part_a = value.astype(BF).astype(F32)
    part_b = (value - part_a).astype(BF).astype(F32)
    part_c = value - part_a - part_b
    weight_map = jnp.zeros((16, 128), F32)
    for part in (part_a, part_b, part_c):
        weight_map = weight_map + dot(jnp.where(hit, part, 0.0).astype(BF), low, NT)

    both = jnp.concatenate([counts, group_counts], axis=0)
    upper = indicator(
        lax.broadcasted_iota(jnp.int32, (128, 128), 0) <= lax.broadcasted_iota(jnp.int32, (128, 128), 1)
    )
    running = dot(both.astype(BF), upper, NN)
    totals = dot(both.astype(BF), jnp.ones((128, 128), BF), NN)
    left = lax.broadcasted_iota(jnp.int32, (32, 32), 0)
    right = lax.broadcasted_iota(jnp.int32, (32, 32), 1)
    before = indicator(((left >> 2) == (right >> 2)) & (right < left))
    rank = running + dot(before, totals.astype(BF), NN) - 1.0
    rank = jnp.where(both > 0.5, rank, -1.0)
    place = lax.broadcasted_iota(jnp.int32, (MOST, 512), 0).astype(F32)

    def line(values, first):
        return jnp.concatenate([values[first + h : first + h + 1, :] for h in range(4)], axis=1)

    for n in range(4):
        pick_out[16 * n : 16 * n + 16, :] = indicator(place == line(rank, 4 * n))
        chosen_here = jnp.where(place == line(rank, 16 + 4 * n), line(weight_map, 4 * n), 0.0)
        weight_out[16 * n : 16 * n + 16, :] = jnp.broadcast_to(
            jnp.sum(chosen_here, axis=1, keepdims=True), (MOST, 128)
        )
    loads[0].wait()
    rows_out[...] = dot(pick_out[...], tok_buf[...], NN).astype(BF)
    loads[1].wait()
    grads_out[...] = dot(pick_out[...], grad_buf[...], NN).astype(BF)


def route(chosen, slot_weight, tokens, out_grad):
    width = tokens.shape[1]
    vmem = pl.BlockSpec(memory_space=pltpu.VMEM)
    return pl.pallas_call(
        route_kernel,
        out_shape=(
            jax.ShapeDtypeStruct((SLOTS, width), BF),
            jax.ShapeDtypeStruct((SLOTS, width), BF),
            jax.ShapeDtypeStruct((SLOTS, tokens.shape[0]), BF),
            jax.ShapeDtypeStruct((SLOTS, 128), F32),
        ),
        in_specs=[vmem, vmem, pl.BlockSpec(memory_space=pl.ANY), pl.BlockSpec(memory_space=pl.ANY)],
        out_specs=(vmem,) * 4,
        scratch_shapes=[
            pltpu.VMEM(tokens.shape, BF),
            pltpu.VMEM(out_grad.shape, BF),
            pltpu.SemaphoreType.DMA((2,)),
        ],
        compiler_params=pltpu.CompilerParams(vmem_limit_bytes=32 * 2**20),
    )(chosen, slot_weight, tokens, out_grad)


def main_kernel(rows_in, grads_in, weight_in, w_gate, w_up, w_down, back_out, final_gu_out, final_d_out,
                wg, wu, wd, rows, raw, gout, rx, rg, rh, hq, ggp, gup, slot_send, back,
                part_gu, part_d, got_gu, got_d, fin_gu, fin_d, fg, fd,
                w_sem, disp_s, disp_r, early_s, early_r, late_s, late_r, ret_s, ret_r,
                sum_s, sum_r, gu_s, gu_r, d_s, d_r):
    dp = lax.axis_index("dp")
    me = lax.axis_index("expert")
    yl = dp % 2
    core = me % 2
    along_x = (dp // 2) % 4
    along_z = dp // 8
    a = along_x + core * (along_z - along_x)
    b = along_z + core * (along_x - along_z)

    def dp_of(a_at, b_at, y_at):
        return a_at * (2 + 6 * core) + b_at * (8 - 6 * core) + y_at

    def remote(src, dst, send_sem, recv_sem, target):
        return pltpu.make_async_remote_copy(
            src_ref=src, dst_ref=dst, send_sem=send_sem, recv_sem=recv_sem,
            device_id=target, device_id_type=MESH,
        )

    weights = []
    for n, (src, dst) in enumerate(((w_gate, wg), (w_up, wu), (w_down, wd))):
        half = dst.shape[0] // 2
        for h in range(2):
            part = pl.ds(h * half, half)
            weights.append(pltpu.make_async_copy(src.at[0, part], dst.at[part], w_sem.at[2 * n + h]))
    for copy in weights:
        copy.start()

    barrier = pltpu.get_barrier_semaphore()

    def greet(target):
        pl.semaphore_signal(barrier, inc=1, device_id=target, device_id_type=MESH)

    for n in range(1, 4):
        greet((dp, (me + n) % 4))
        greet((dp_of((a + n) % 4, b, yl), me))
        greet((dp_of((a + n) % 4, b, 1 - yl), me))
        greet((dp_of(a, (b + n) % 4, yl), me))
    greet((dp_of(a, b, 1 - yl), me))

    gu_sources = [dp_of(j, (dp % 16) // 4, dp // 16) for j in range(4)]
    d_sources = [dp_of(dp // 8, n % 4, n // 4) for n in range(8)]
    for source in gu_sources + d_sources:
        greet((source, me))
    pl.semaphore_wait(barrier, 25)

    block = lambda n: pl.ds(MOST * n, MOST)
    dispatch = [[], []]
    for which, (src, dst) in enumerate(((rows_in, rows), (grads_in, raw))):
        for n in (2, 1, 3):
            copy = remote(
                src.at[block(n)], dst.at[block(n)], disp_s.at[which, n], disp_r.at[which, n],
                (dp, (me + n) % 4),
            )
            copy.start()
            dispatch[which].append(copy)
    rows[0:MOST, :] = rows_in[0:MOST, :]
    raw[0:MOST, :] = grads_in[0:MOST, :]

    width = rows.shape[1]
    half = width // 2
    mine = pl.ds(pl.multiple_of(yl * half, half), half)
    other = pl.ds(pl.multiple_of((1 - yl) * half, half), half)
    slot = lambda y, d: pl.ds(SLOTS * (4 * y + d), SLOTS)

    def early_sends(which, src, dst):
        copies = [remote(
            src.at[:, other], dst.at[slot(1, 0)], early_s.at[which, 0], early_r.at[which, 0],
            (dp_of(a, b, 1 - yl), me),
        )]
        for n in (2, 1, 3):
            copies.append(remote(
                src.at[:, mine], dst.at[slot(0, n)], early_s.at[which, n], early_r.at[which, n],
                (dp_of((a + n) % 4, b, yl), me),
            ))
        for copy in copies:
            copy.start()
        dst[0:SLOTS, :] = src[:, mine]
        return copies

    def forward_sends(which, dst):
        copies = []
        for n in (2, 1, 3):
            copy = remote(
                dst.at[slot(1, 0)], dst.at[slot(1, n)], early_s.at[which, 3 + n], early_r.at[which, 3 + n],
                (dp_of((a + n) % 4, b, yl), me),
            )
            copy.start()
            copies.append(copy)
        return copies

    for copy in dispatch[0]:
        copy.wait_recv()
    early = early_sends(0, rows, rx)
    for copy in weights[0:4]:
        copy.wait()
    gate_pre = dot(rows[...], wg[...], NN)
    up_pre = dot(rows[...], wu[...], NN)
    for copy in dispatch[1]:
        copy.wait_recv()
    gout[...] = (weight_in[:, 0:1] * raw[...].astype(F32)).astype(BF)
    early_g = early_sends(1, gout, rg)
    sig = 1.0 / (1.0 + jnp.exp(-gate_pre))
    activated = gate_pre * sig
    hidden = (activated * up_pre).astype(BF)
    early[0].wait_recv()
    forwards = forward_sends(0, rx)
    for copy in weights[4:6]:
        copy.wait()
    grad_hidden = dot(gout[...], wd[...], NT)
    ggp[...] = (grad_hidden * up_pre * (sig * (1.0 + gate_pre * (1.0 - sig)))).astype(BF)
    gup[...] = (grad_hidden * activated).astype(BF)
    blank = jnp.zeros((SLOTS, QPAD - QUARTER), BF)
    for n, value in enumerate((ggp[...], gup[...], hidden)):
        for j in range(4):
            hq[j, :, QPAD * n : QPAD * (n + 1)] = jnp.concatenate(
                [value[:, QUARTER * j : QUARTER * (j + 1)], blank], axis=1
            )

    late = []
    for y, n in ((1, 2), (1, 1), (1, 3), (1, 0), (0, 2), (0, 1), (0, 3)):
        at = (a + n) % 4
        copy = remote(
            hq.at[at], rh.at[slot(y, n)], late_s.at[4 * y + n], late_r.at[4 * y + n],
            (dp_of(at, b, yl + y * (1 - 2 * yl)), me),
        )
        copy.start()
        late.append(copy)
    rh[0:SLOTS, :] = hq[a]
    early_g[0].wait_recv()
    forwards += forward_sends(1, rg)

    slot_grad = dot(ggp[...], wg[...], NT) + dot(gup[...], wu[...], NT)
    slot_send[...] = slot_grad.astype(BF)
    returns = []
    for n in (2, 1, 3):
        copy = remote(
            slot_send.at[block(n)], back.at[block(n)], ret_s.at[n], ret_r.at[n],
            (dp, (me + 4 - n) % 4),
        )
        copy.start()
        returns.append(copy)
    back[0:MOST, :] = slot_send[0:MOST, :]

    for copy in early[1:] + early_g[1:] + forwards + late:
        copy.wait_recv()

    chunk = half // 4
    sums = []
    for n in (2, 1, 3, 0):
        at = (b + n) % 4
        columns = pl.ds(pl.multiple_of(at * chunk, chunk), chunk)
        part_gu[n] = dot(rx[:, columns], rh[:, 0 : 2 * QPAD], TN).astype(BF)
        part_d[n] = dot(rh[:, 2 * QPAD : 3 * QPAD], rg[:, columns], TN).astype(BF)
        if n:
            target = (dp_of(a, at, yl), me)
            for which, (src, dst) in enumerate(((part_gu, got_gu), (part_d, got_d))):
                copy = remote(
                    src.at[n], dst.at[n], sum_s.at[which, n], sum_r.at[which, n], target
                )
                copy.start()
                sums.append(copy)

    for copy in returns:
        copy.wait_recv()
    back_out[...] = back[...]

    for copy in sums:
        copy.wait_recv()
    scale = 1.0 / 32
    total = part_gu[0].astype(F32)
    for n in range(1, 4):
        total = total + got_gu[n].astype(F32)
    fin_gu[...] = (total * scale).astype(BF)
    total = part_d[0].astype(F32)
    for n in range(1, 4):
        total = total + got_d[n].astype(F32)
    total = total * scale
    spare = jnp.zeros((4, chunk), F32)
    for m in range(8):
        fin_d[m] = jnp.concatenate([total[44 * m : 44 * m + 44, :], spare], axis=0).astype(BF)

    def place(src, dst, send_sem, recv_sem, owner):
        copy = remote(src, dst, send_sem, recv_sem, (owner, me))

        @pl.when(owner != dp)
        def _():
            copy.start()

        @pl.when(owner == dp)
        def _():
            pltpu.make_async_copy(src, dst, recv_sem).start()

        return owner, copy

    placed = []
    for m in range(4):
        placed.append(place(
            fin_gu.at[pl.ds(64 * m, 64)], fg.at[a], gu_s.at[m], gu_r.at[a], 16 * yl + 4 * b + m
        ))
    for m in range(8):
        placed.append(place(
            fin_d.at[m], fd.at[4 * yl + b], d_s.at[m], d_r.at[4 * yl + b], 8 * a + m
        ))
    for j in range(4):
        pltpu.make_async_copy(fg.at[j], fg.at[j], gu_r.at[j]).wait()
    for n in range(8):
        pltpu.make_async_copy(fd.at[n], fd.at[n], d_r.at[n]).wait()
    final_gu_out[...] = fg[...]
    final_d_out[...] = fd[...]

    for copy in dispatch[0] + dispatch[1] + early + early_g + forwards + late + returns + sums:
        copy.wait_send()
    for owner, copy in placed:
        @pl.when(owner != dp)
        def _():
            copy.wait_send()


def main_pass(rows, grads, weights, w_gate, w_up, w_down):
    width = rows.shape[1]
    hid = w_gate.shape[2]
    half = width // 2
    chunk = half // 4
    vmem = pl.BlockSpec(memory_space=pltpu.VMEM)
    hbm = pl.BlockSpec(memory_space=pl.ANY)
    dma = pltpu.SemaphoreType.DMA
    return pl.pallas_call(
        main_kernel,
        out_shape=(
            jax.ShapeDtypeStruct((SLOTS, width), BF),
            jax.ShapeDtypeStruct((4, 64, 2 * QPAD), BF),
            jax.ShapeDtypeStruct((8, 48, chunk), BF),
        ),
        in_specs=[vmem, vmem, vmem, hbm, hbm, hbm],
        out_specs=(vmem,) * 3,
        scratch_shapes=[
            pltpu.VMEM((width, hid), BF),
            pltpu.VMEM((width, hid), BF),
            pltpu.VMEM((hid, width), BF),
            pltpu.VMEM((SLOTS, width), BF),
            pltpu.VMEM((SLOTS, width), BF),
            pltpu.VMEM((SLOTS, width), BF),
            pltpu.VMEM((8 * SLOTS, half), BF),
            pltpu.VMEM((8 * SLOTS, half), BF),
            pltpu.VMEM((8 * SLOTS, 3 * QPAD), BF),
            pltpu.VMEM((4, SLOTS, 3 * QPAD), BF),
            pltpu.VMEM((SLOTS, hid), BF),
            pltpu.VMEM((SLOTS, hid), BF),
            pltpu.VMEM((SLOTS, width), BF),
            pltpu.VMEM((SLOTS, width), BF),
            pltpu.VMEM((4, chunk, 2 * QPAD), BF),
            pltpu.VMEM((4, QPAD, chunk), BF),
            pltpu.VMEM((4, chunk, 2 * QPAD), BF),
            pltpu.VMEM((4, QPAD, chunk), BF),
            pltpu.VMEM((chunk, 2 * QPAD), BF),
            pltpu.VMEM((8, 48, chunk), BF),
            pltpu.VMEM((4, 64, 2 * QPAD), BF),
            pltpu.VMEM((8, 48, chunk), BF),
            dma((6,)),
            dma((2, 4)), dma((2, 4)),
            dma((2, 7)), dma((2, 7)),
            dma((8,)), dma((8,)),
            dma((4,)), dma((4,)),
            dma((2, 4)), dma((2, 4)),
            dma((4,)), dma((4,)),
            dma((8,)), dma((8,)),
        ],
        compiler_params=pltpu.CompilerParams(
            collective_id=0, has_side_effects=True, vmem_limit_bytes=56 * 2**20
        ),
    )(rows, grads, weights, w_gate, w_up, w_down)


def finish_kernel(pick, back, final_gu, final_d, token_grad, grad_gate, grad_up, grad_down):
    for n in range(4):
        part = pl.ds(128 * n, 128)
        token_grad[part, :] = dot(pick[:, part], back[...], TN).astype(BF)
    for j in range(4):
        grad_gate[0, :, QUARTER * j : QUARTER * (j + 1)] = final_gu[j, :, 0:QUARTER]
        grad_up[0, :, QUARTER * j : QUARTER * (j + 1)] = final_gu[j, :, QPAD : QPAD + QUARTER]
    for n in range(8):
        grad_down[0, :, 256 * n : 256 * (n + 1)] = final_d[n, 0:44, :]


def finish(pick, back, final_gu, final_d, hid):
    width = back.shape[1]
    vmem = pl.BlockSpec(memory_space=pltpu.VMEM)
    return pl.pallas_call(
        finish_kernel,
        out_shape=(
            jax.ShapeDtypeStruct((pick.shape[1], width), BF),
            jax.ShapeDtypeStruct((1, width // 32, hid), BF),
            jax.ShapeDtypeStruct((1, width // 32, hid), BF),
            jax.ShapeDtypeStruct((1, hid // 32, width), BF),
        ),
        in_specs=[vmem] * 4,
        out_specs=(vmem,) * 4,
        compiler_params=pltpu.CompilerParams(vmem_limit_bytes=32 * 2**20),
    )(pick, back, final_gu, final_d)


def local(tokens, out_grad, chosen, slot_weight, w_gate, w_up, w_down):
    rows, grads, pick, weights = route(chosen, slot_weight, tokens, out_grad)
    back, final_gu, final_d = main_pass(rows, grads, weights, w_gate, w_up, w_down)
    return finish(pick, back, final_gu, final_d, w_gate.shape[2])


def solution(mesh):
    return jax.shard_map(
        local,
        mesh=mesh,
        in_specs=(
            P(("dp", "expert"), None),
            P(("dp", "expert"), None),
            P(),
            P("expert", None),
            P("expert", None, None),
            P("expert", None, None),
            P("expert", None, None),
        ),
        out_specs=(
            P(("dp", "expert"), None),
            P("expert", "dp", None),
            P("expert", "dp", None),
            P("expert", "dp", None),
        ),
        check_vma=False,
    )
```

time: 494 us -> 79.5 us (0.16)
  blocking collectives: 256 us -> 0 us
  waiting for transfers between devices: 137 us -> 0 us
  Pallas kernels: 0 us -> 68 us
  matrix products: 34.4 us -> 0 us
  starting transfers between devices: 21.5 us -> 0 us
  other arithmetic: 18.7 us -> 0 us
  between operations: 14.9 us -> 0.68 us
    unnamed x1 -> x0, blocking collectives: 256 us -> none
    reduce_scatter x2 -> x0, waiting for transfers between devices: 131 us -> none  [the longest x1 131 us: local(): lax.psum_scatter(part_up.astype(jnp.bfloat16), 'dp', scatter_dimension=0,...]
    pallas_call x0 -> x3, Pallas kernels: none -> 68 us  [the longest x1 63.5 us: main_pass(): pl.pallas_call(main_kernel, out_shape=(jax.ShapeDtypeStruct((SLOTS, width...]
    dot_general x8 -> x0, matrix products: 34.4 us -> none  [the longest x3 12.6 us: contract_rows(): lax.dot_general(left_rows, right_rows, (((0,), (0,)), ((), ())), preferre...]
    all_to_all x3 -> x0, starting transfers between devices: 12.6 us -> none  [the longest x1 4.66 us: local(): lax.all_to_all(send_back.astype(jnp.bfloat16), 'expert', split_axis=0, co...]
    unnamed x3 -> x0, starting transfers between devices: 8.76 us -> none
    unnamed x18 -> x20, local copies, waits for them, and re-layouts: 2.47 us -> 9.44 us
    all_to_all x3 -> x0, waiting for transfers between devices: 6.42 us -> none  [the longest x1 6.39 us: local(): lax.all_to_all(send_tokens, 'expert', split_axis=0, concat_axis=0, tiled=...]
  transfers between devices with their start and end apart: 8 -> 0, of which waited for: 2 -> 0; matrix products, arithmetic and copies ran while one was open for 60% -> 0% of each run, Pallas kernels for 0% -> 0%
where the time goes in v1:
time: 79.5 us; the launch traced here: 78.1 us
  Pallas kernels  68 us (86%)
  local copies, waits for them, and re-layouts  9.44 us (12%)
    pallas_call x1, Pallas kernels, main_pass(): pl.pallas_call(main_kernel, out_shape=(jax.ShapeDtypeStruct((SLOTS, width...  63.5 us
    unnamed x20, local copies, waits for them, and re-layouts  9.44 us
    pallas_call x1, Pallas kernels, route(): pl.pallas_call(route_kernel, out_shape=(jax.ShapeDtypeStruct((SLOTS, widt...  2.29 us
    pallas_call x1, Pallas kernels, finish(): pl.pallas_call(finish_kernel, out_shape=(jax.ShapeDtypeStruct((pick.shape...  2.18 us

profile of v1, /device:TPU:0, one launch (start us, length us, event | category | flops | bytes accessed | tf_op | source)
XLA Modules:
  0.0 78.1 jit_solution(7550895399202589187)
XLA Ops:
  0.6 0.0 copy-start
  0.6 1.6 %copy-done = bf16[512,2048]{1,0:T(8,128)(2,1)S(1)} copy-done((bf16[512,2048]{1,0:T(8,128)(2,1)S(1)}, bf16[512,2048]{1,0:T(8,128)(2,1)}, u32[]{:S(2)}) %copy-start) | copy-done | bytes 2097176
  2.2 0.0 copy-start.1
  2.2 1.6 %copy-done.1 = bf16[512,2048]{1,0:T(8,128)(2,1)S(1)} copy-done((bf16[512,2048]{1,0:T(8,128)(2,1)S(1)}, bf16[512,2048]{1,0:T(8,128)(2,1)}, u32[]{:S(2)}) %copy-start.1) | copy-done | bytes 2097176
  3.8 0.0 copy-start.8
  3.8 0.7 copy-done.8
  4.5 0.0 copy-start.9
  4.5 0.7 copy-done.9
  5.2 2.3 %shard_map.102 = (bf16[64,2048]{1,0:T(8,128)(2,1)S(1)}, bf16[64,2048]{1,0:T(8,128)(2,1)S(1)}, bf16[64,512]{1,0:T(8,128)(2,1)S(1)}, f32[64,128]{1,0:T(8,128)S(1)}) custom-call(s32[4,1024]{1,0:T(4,128)S(1)} %copy-done.8, f32[1,1024]{1,0:T(1,128)S(1)} %copy-done.9, bf16[512,2048]{1,0:T(8,128)(2,1)S(1)} %copy-done, bf16[512,2048]{1,0:T(8,128)(2,1)S(1)} %copy-done.1), custom_call_target="tpu_custom_call" | custom-call | tf_op jit(solution)/shard_map/pallas_call | solution.py:94
  7.5 0.0 copy-start.3
  7.5 0.7 copy-done.3
  8.2 0.0 copy-start.4
  8.2 0.7 copy-done.4
  8.9 0.0 copy-start.7
  8.9 0.6 copy-done.7
  9.5 63.5 %shard_map.103 = (bf16[64,2048]{1,0:T(8,128)(2,1)}, bf16[4,64,768]{2,1,0:T(8,128)(2,1)}, bf16[8,48,256]{2,1,0:T(8,128)(2,1)}) custom-call(bf16[64,2048]{1,0:T(8,128)(2,1)} %copy-done.3, bf16[64,2048]{1,0:T(8,128)(2,1)} %copy-done.4, f32[64,128]{1,0:T(8,128)} %copy-done.7, bf16[1,2048,1408]{2,1,0:T(8,128)(2,1)} %w_gate.1, bf16[1,2048,1408]{2,1,0:T(8,128)(2,1)} %w_up.1, ...), custom_call_target="tpu_custom_call" | custom-call | tf_op jit(solution)/shard_map/pallas_call | solution.py:344
  73.1 0.0 copy-start.2
  73.1 1.0 %copy-done.2 = bf16[4,64,768]{2,1,0:T(8,128)(2,1)S(1)} copy-done((bf16[4,64,768]{2,1,0:T(8,128)(2,1)S(1)}, bf16[4,64,768]{2,1,0:T(8,128)(2,1)}, u32[]{:S(2)}) %copy-start.2) | copy-done | bytes 393240
  74.1 0.0 copy-start.5
  74.1 0.9 %copy-done.5 = bf16[64,2048]{1,0:T(8,128)(2,1)S(1)} copy-done((bf16[64,2048]{1,0:T(8,128)(2,1)S(1)}, bf16[64,2048]{1,0:T(8,128)(2,1)}, u32[]{:S(2)}) %copy-start.5) | copy-done | bytes 262168
  75.0 0.0 copy-start.6
  75.0 0.9 %copy-done.6 = bf16[8,48,256]{2,1,0:T(8,128)(2,1)S(1)} copy-done((bf16[8,48,256]{2,1,0:T(8,128)(2,1)S(1)}, bf16[8,48,256]{2,1,0:T(8,128)(2,1)}, u32[]{:S(2)}) %copy-start.6) | copy-done | bytes 196632
  75.9 2.2 %shard_map.104 = (bf16[512,2048]{1,0:T(8,128)(2,1)}, bf16[1,64,1408]{2,1,0:T(8,128)(2,1)}, bf16[1,64,1408]{2,1,0:T(8,128)(2,1)}, bf16[1,44,2048]{2,1,0:T(8,128)(2,1)}) custom-call(bf16[64,512]{1,0:T(8,128)(2,1)S(1)} %get-tuple-element.11.pick, bf16[64,2048]{1,0:T(8,128)(2,1)S(1)} %copy-done.5, bf16[4,64,768]{2,1,0:T(8,128)(2,1)S(1)} %copy-done.2, ...), custom_call_target="tpu_custom_call" | custom-call | tf_op jit(solution)/shard_map/pallas_call | solution.py:405
Async XLA Ops:
  0.6 1.6 %copy-start = (bf16[512,2048]{1,0:T(8,128)(2,1)S(1)}, bf16[512,2048]{1,0:T(8,128)(2,1)}, u32[]{:S(2)}) copy-start(bf16[512,2048]{1,0:T(8,128)(2,1)} %tokens.1) | copy-start | bytes 6291460
  2.2 1.6 %copy-start.1 = (bf16[512,2048]{1,0:T(8,128)(2,1)S(1)}, bf16[512,2048]{1,0:T(8,128)(2,1)}, u32[]{:S(2)}) copy-start(bf16[512,2048]{1,0:T(8,128)(2,1)} %out_grad.1) | copy-start | bytes 6291460
  3.8 0.7 copy-start.8
  4.5 0.7 copy-start.9
  7.5 0.7 copy-start.3
  8.2 0.7 copy-start.4
  8.9 0.6 copy-start.7
  73.1 1.0 %copy-start.2 = (bf16[4,64,768]{2,1,0:T(8,128)(2,1)S(1)}, bf16[4,64,768]{2,1,0:T(8,128)(2,1)}, u32[]{:S(2)}) copy-start(bf16[4,64,768]{2,1,0:T(8,128)(2,1)} %get-tuple-element.16.final_gu) | copy-start | bytes 1179652
  74.1 0.9 %copy-start.5 = (bf16[64,2048]{1,0:T(8,128)(2,1)S(1)}, bf16[64,2048]{1,0:T(8,128)(2,1)}, u32[]{:S(2)}) copy-start(bf16[64,2048]{1,0:T(8,128)(2,1)} %get-tuple-element.15.back) | copy-start | bytes 786436
  75.0 0.9 %copy-start.6 = (bf16[8,48,256]{2,1,0:T(8,128)(2,1)S(1)}, bf16[8,48,256]{2,1,0:T(8,128)(2,1)}, u32[]{:S(2)}) copy-start(bf16[8,48,256]{2,1,0:T(8,128)(2,1)} %get-tuple-element.17.final_d) | copy-start | bytes 589828

commit v2 on v0

v2 whole, which is shorter than its diff:
```python
import jax
import jax.numpy as jnp
from jax import lax
from jax.experimental import pallas as pl
from jax.experimental.pallas import tpu as pltpu
from jax.sharding import PartitionSpec as P

MESH = pl.DeviceIdType.MESH
BF = jnp.bfloat16
F32 = jnp.float32
MOST = 16
SLOTS = 64
QUARTER = 352
QPAD = 384
NN = (((1,), (0,)), ((), ()))
NT = (((1,), (1,)), ((), ()))
TN = (((0,), (0,)), ((), ()))


def dot(lhs, rhs, dims):
    return lax.dot_general(lhs, rhs, dims, preferred_element_type=F32)


def indicator(cond):
    return jnp.where(cond, 1.0, 0.0).astype(BF)


def route(me, dp, chosen, slot_weight, pick, weight):
    slots = chosen.shape[1]
    row = lax.broadcasted_iota(jnp.int32, (16, slots), 0)
    low_iota = lax.broadcasted_iota(jnp.int32, (128, slots), 0)
    lists = chosen[...]
    counts = jnp.zeros((16, 128), F32)
    group_counts = jnp.zeros((16, 128), F32)
    weight_map = jnp.zeros((16, 128), F32)
    value = slot_weight[...]
    part_a = value.astype(BF).astype(F32)
    part_b = (value - part_a).astype(BF).astype(F32)
    part_c = value - part_a - part_b
    for f in range(4):
        entries = lists[f : f + 1, :]
        low = indicator(low_iota == (entries & 127))
        tile = entries >> 7
        high = tile - (dp * 4 + me) * 4
        n = (f + 4 - me) % 4
        high = jnp.where((high >= 0) & (high < 4), high + 4 * n, -1)
        counts = counts + dot(indicator(row == high), low, NT)
        if f == 0:
            mine, mine_low = tile, low
        else:
            is_mine = me == f
            mine = jnp.where(is_mine, tile, mine)
            mine_low = jnp.where(is_mine, low, mine_low)
    wanted = 4 * ((me + 4 - (row >> 2)) & 3) + (row & 3)
    hit = wanted == mine - dp * 16
    stacked = jnp.concatenate(
        [jnp.where(hit, part, 0.0).astype(BF) for part in (jnp.ones_like(value), part_a, part_b, part_c)],
        axis=0,
    )
    found = dot(stacked, mine_low, NT)
    group_counts = found[0:16]
    weight_map = found[16:32] + found[32:48] + found[48:64]

    both = jnp.concatenate([counts, group_counts], axis=0)
    upper = indicator(
        lax.broadcasted_iota(jnp.int32, (128, 128), 0) <= lax.broadcasted_iota(jnp.int32, (128, 128), 1)
    )
    running = dot(both.astype(BF), upper, NN)
    totals = dot(both.astype(BF), jnp.ones((128, 128), BF), NN)
    left = lax.broadcasted_iota(jnp.int32, (32, 32), 0)
    right = lax.broadcasted_iota(jnp.int32, (32, 32), 1)
    before = indicator(((left >> 2) == (right >> 2)) & (right < left))
    rank = running + dot(before, totals.astype(BF), NN) - 1.0
    rank = jnp.where(both > 0.5, rank, -1.0)
    place = lax.broadcasted_iota(jnp.int32, (MOST, 512), 0).astype(F32)

    def line(values, first):
        return jnp.concatenate([values[first + h : first + h + 1, :] for h in range(4)], axis=1)

    for n in range(4):
        pick[16 * n : 16 * n + 16, :] = indicator(place == line(rank, 4 * n))
        chosen_here = jnp.where(place == line(rank, 16 + 4 * n), line(weight_map, 4 * n), 0.0)
        weight[16 * n : 16 * n + 16, :] = jnp.broadcast_to(
            jnp.sum(chosen_here, axis=1, keepdims=True), (MOST, 128)
        )


def main_kernel(chosen, slot_weight, tokens, out_grad, w_gate, w_up, w_down,
                pick, back, fin_g, fin_u, fin_d,
                tok_buf, grad_buf, weight, rows_in, grads_in, wg, wu, wd, rows, raw, gout, xh, gh, rx, rg,
                rh, hq, ggp, gup, slot_send, back_buf, part_d, got_d, part_gu, got_gu, out_d, out_gu,
                land_d, land_gu,
                load_sem, w_sem, disp_s, disp_r, early_s, early_r, late_s, late_r, cross_s, cross_r,
                ret_s, ret_r, sum_s, sum_r, put_s, put_r):
    dp = lax.axis_index("dp")
    me = lax.axis_index("expert")
    yl = dp % 2
    core = me % 2
    along_x = (dp // 2) % 4
    along_z = dp // 8
    a = along_x + core * (along_z - along_x)
    b = along_z + core * (along_x - along_z)

    def at_dp(a_at, b_at, y_at):
        return a_at * (2 + 6 * core) + b_at * (8 - 6 * core) + y_at

    ring_a = [(at_dp((a + n) % 4, b, yl), me) for n in range(4)]
    ring_b = [(at_dp(a, (b + n) % 4, yl), me) for n in range(4)]
    across = (at_dp(a, b, 1 - yl), me)
    started = []

    def send(src, dst, send_sem, recv_sem, target):
        copy = pltpu.make_async_remote_copy(
            src_ref=src, dst_ref=dst, send_sem=send_sem, recv_sem=recv_sem,
            device_id=target, device_id_type=MESH,
        )
        copy.start()
        started.append(copy)
        return copy

    loads = [
        pltpu.make_async_copy(tokens, tok_buf, load_sem.at[0]),
        pltpu.make_async_copy(out_grad, grad_buf, load_sem.at[1]),
    ]
    weights = []
    for n, (src, dst) in enumerate(((w_gate, wg), (w_up, wu), (w_down, wd))):
        half = dst.shape[0] // 2
        for h in range(2):
            part = pl.ds(h * half, half)
            weights.append(pltpu.make_async_copy(src.at[0, part], dst.at[part], w_sem.at[2 * n + h]))
    for copy in loads + weights:
        copy.start()

    barrier = pltpu.get_barrier_semaphore()
    friends = [(dp, (me + n) % 4) for n in range(1, 4)] + ring_a[1:] + ring_b[1:] + [across]
    for friend in friends:
        pl.semaphore_signal(barrier, inc=1, device_id=friend, device_id_type=MESH)

    route(me, dp, chosen, slot_weight, pick, weight)
    loads[0].wait()
    rows_in[...] = dot(pick[...], tok_buf[...], NN).astype(BF)
    pl.semaphore_wait(barrier, len(friends))

    block = lambda n: pl.ds(MOST * n, MOST)

    def dispatch(which, src, dst):
        copies = [
            send(src.at[block(n)], dst.at[block(n)], disp_s.at[which, n], disp_r.at[which, n],
                 (dp, (me + n) % 4))
            for n in (2, 3, 1)
        ]
        dst[0:MOST, :] = src[0:MOST, :]
        return copies

    row_copies = dispatch(0, rows_in, rows)
    loads[1].wait()
    grads_in[...] = dot(pick[...], grad_buf[...], NN).astype(BF)
    grad_copies = dispatch(1, grads_in, raw)

    half = rows.shape[1] // 2
    slot = lambda y, d: pl.ds(SLOTS * (4 * y + d), SLOTS)

    def early_sends(which, src, dst):
        copies = [send(src.at[1 - yl], dst.at[slot(1, 0)], early_s.at[which, 0], early_r.at[which, 0], across)]
        for n in (2, 1, 3):
            copies.append(send(
                src.at[yl], dst.at[slot(0, n)], early_s.at[which, n], early_r.at[which, n], ring_a[n]
            ))
        dst[0:SLOTS, :] = src[yl]
        return copies

    def early_forward(which, dst):
        return [
            send(dst.at[slot(1, 0)], dst.at[slot(1, n)], early_s.at[which, 3 + n],
                 early_r.at[which, 3 + n], ring_a[n])
            for n in (2, 1, 3)
        ]

    for copy in row_copies:
        copy.wait_recv()
    for which in range(2):
        @pl.when(core == which)
        def _():
            for y in range(2):
                order = [u if which == 0 else 4 * (u % 4) + u // 4 for u in range(16)]
                xh[y] = jnp.concatenate(
                    [rows[:, 128 * u + 64 * y : 128 * u + 64 * y + 64] for u in order], axis=1
                )
    early_x = early_sends(0, xh, rx)

    for copy in weights[0:4]:
        copy.wait()
    gate_pre = dot(rows[...], wg[...], NN)
    up_pre = dot(rows[...], wu[...], NN)
    sig = 1.0 / (1.0 + jnp.exp(-gate_pre))
    activated = gate_pre * sig
    ggp[...] = (activated * up_pre).astype(BF)
    gap = jnp.zeros((SLOTS, 4), BF)
    for which in range(2):
        @pl.when(core == which)
        def _():
            for j in range(4):
                pieces = []
                for v in range(8):
                    owner = (v // 2) * 8 + 2 * j + v % 2 if which == 0 else 8 * j + v
                    pieces += [ggp[:, 44 * owner : 44 * owner + 44], gap]
                hq[0, j] = jnp.concatenate(pieces, axis=1)

    def late_sends(part):
        copies = [None] + [
            send(hq.at[part, (a + n) % 4], rh.at[part, slot(0, n)], late_s.at[part, n], late_r.at[part, n],
                 ring_a[n])
            for n in (1, 2, 3)
        ]
        rh[part, 0:SLOTS, :] = hq[part, a]
        crossed = [send(hq.at[part, a], rh.at[part, slot(1, 0)], cross_s.at[part, 0], cross_r.at[part, 0], across)]
        return copies, crossed

    def late_cross(part, copies):
        crossed = []
        for n in (1, 3, 2):
            copies[n].wait_recv()
            crossed.append(send(
                rh.at[part, slot(0, n)], rh.at[part, slot(1, n)], cross_s.at[part, n], cross_r.at[part, n], across
            ))
        return crossed

    late = [None] * 3
    crossed = [None] * 3
    late[0], crossed[0] = late_sends(0)

    for copy in grad_copies:
        copy.wait_recv()
    gout[...] = (weight[:, 0:1] * raw[...].astype(F32)).astype(BF)
    for y in range(2):
        gh[y] = gout[:, half * y : half * (y + 1)]
    early_g = early_sends(1, gh, rg)
    early_x[0].wait_recv()
    early_x += early_forward(0, rx)

    for copy in weights[4:6]:
        copy.wait()
    grad_hidden = dot(gout[...], wd[...], NT)
    gup[...] = (grad_hidden * activated).astype(BF)
    ggp[...] = (grad_hidden * up_pre * (sig * (1.0 + gate_pre * (1.0 - sig)))).astype(BF)
    blank = jnp.zeros((SLOTS, QPAD - QUARTER), BF)
    for part, value in ((1, gup), (2, ggp)):
        for j in range(4):
            hq[part, j] = jnp.concatenate([value[:, QUARTER * j : QUARTER * (j + 1)], blank], axis=1)
        late[part], crossed[part] = late_sends(part)
    crossed[0] += late_cross(0, late[0])
    early_g[0].wait_recv()
    early_g += early_forward(1, rg)
    crossed[1] += late_cross(1, late[1])
    crossed[2] += late_cross(2, late[2])

    slot_grad = dot(ggp[...], wg[...], NT) + dot(gup[...], wu[...], NT)
    slot_send[...] = slot_grad.astype(BF)
    returns = [
        send(slot_send.at[block(n)], back_buf.at[block(n)], ret_s.at[n], ret_r.at[n], (dp, (me + 4 - n) % 4))
        for n in (2, 1, 3)
    ]
    back_buf[0:MOST, :] = slot_send[0:MOST, :]

    chunk = half // 4
    sums = [[], [], []]
    for copy in early_g[1:] + crossed[0]:
        copy.wait_recv()
    part_d[...] = dot(rh[0], rg[...], TN).astype(BF)
    rows_d = QPAD // 4
    for n in (2, 1, 3):
        sums[0].append(send(
            part_d.at[pl.ds(pl.multiple_of((b + n) % 4 * rows_d, rows_d), rows_d)], got_d.at[n],
            sum_s.at[0, n], sum_r.at[0, n], ring_b[n],
        ))
    for copy in early_x[1:]:
        copy.wait_recv()
    for part in (1, 2):
        for copy in crossed[part]:
            copy.wait_recv()
        for n in (2, 1, 3, 0):
            columns = pl.ds(pl.multiple_of((b + n) % 4 * chunk, chunk), chunk)
            part_gu[part - 1, n] = dot(rx[:, columns], rh[part], TN).astype(BF)
            if n:
                sums[part].append(send(
                    part_gu.at[part - 1, n], got_gu.at[part - 1, n],
                    sum_s.at[part, n], sum_r.at[part, n], ring_b[n],
                ))

    scale = 1.0 / 32
    for copy in sums[0]:
        copy.wait_recv()
    total = part_d[pl.ds(pl.multiple_of(b * rows_d, rows_d), rows_d), :].astype(F32)
    for n in range(1, 4):
        total = total + got_d[n].astype(F32)
    out_d[...] = (total * scale).astype(BF).reshape(out_d.shape)
    put_d = send(out_d.at[1 - yl], land_d.at[yl], put_s.at[0, 0], put_r.at[0, 0], across)
    land_d[yl] = out_d[yl]
    puts = []
    for part in (1, 2):
        for copy in sums[part]:
            copy.wait_recv()
        total = part_gu[part - 1, 0].astype(F32)
        for n in range(1, 4):
            total = total + got_gu[part - 1, n].astype(F32)
        out_gu[part - 1] = (total * scale).astype(BF).reshape(out_gu.shape[1:])
        for n in (2, 1, 3):
            puts.append(send(
                out_gu.at[part - 1, (a + n) % 4], land_gu.at[part - 1, a], put_s.at[part, n], put_r.at[part, n],
                ring_a[n],
            ))
        land_gu[part - 1, a] = out_gu[part - 1, a]

    for copy in returns:
        copy.wait_recv()
    back[...] = back_buf[...]
    pltpu.make_async_copy(land_d.at[1 - yl], land_d.at[1 - yl], put_r.at[0, 0]).wait()
    fin_d[...] = land_d[...]
    for part, dst in ((1, fin_u), (2, fin_g)):
        for n in (1, 2, 3):
            there = land_gu.at[part - 1, (a + 4 - n) % 4]
            pltpu.make_async_copy(there, there, put_r.at[part, n]).wait()
        dst[...] = land_gu[part - 1]
    for copy in started:
        copy.wait_send()


def main_pass(chosen, slot_weight, tokens, out_grad, w_gate, w_up, w_down):
    width = tokens.shape[1]
    hid = w_gate.shape[2]
    half = width // 2
    chunk = half // 4
    vmem = pl.BlockSpec(memory_space=pltpu.VMEM)
    hbm = pl.BlockSpec(memory_space=pl.ANY)
    dma = pltpu.SemaphoreType.DMA

    def buf(*shape):
        return pltpu.VMEM(shape, BF)

    return pl.pallas_call(
        main_kernel,
        out_shape=(
            jax.ShapeDtypeStruct((SLOTS, tokens.shape[0]), BF),
            jax.ShapeDtypeStruct((SLOTS, width), BF),
            jax.ShapeDtypeStruct((4, 64, QPAD), BF),
            jax.ShapeDtypeStruct((4, 64, QPAD), BF),
            jax.ShapeDtypeStruct((2, 48, half), BF),
        ),
        in_specs=[vmem, vmem, hbm, hbm, hbm, hbm, hbm],
        out_specs=(vmem,) * 5,
        scratch_shapes=[
            buf(*tokens.shape), buf(*tokens.shape),
            pltpu.VMEM((SLOTS, 128), F32),
            buf(SLOTS, width), buf(SLOTS, width),
            buf(width, hid), buf(width, hid), buf(hid, width),
            buf(SLOTS, width), buf(SLOTS, width), buf(SLOTS, width),
            buf(2, SLOTS, half), buf(2, SLOTS, half),
            buf(8 * SLOTS, half), buf(8 * SLOTS, half),
            buf(3, 8 * SLOTS, QPAD), buf(3, 4, SLOTS, QPAD),
            buf(SLOTS, hid), buf(SLOTS, hid),
            buf(SLOTS, width), buf(SLOTS, width),
            buf(QPAD, half), buf(4, QPAD // 4, half),
            buf(2, 4, chunk, QPAD), buf(2, 4, chunk, QPAD),
            buf(2, 48, half), buf(2, 4, 64, QPAD),
            buf(2, 48, half), buf(2, 4, 64, QPAD),
            dma((2,)), dma((6,)),
            dma((2, 4)), dma((2, 4)),
            dma((2, 7)), dma((2, 7)),
            dma((3, 4)), dma((3, 4)),
            dma((3, 4)), dma((3, 4)),
            dma((4,)), dma((4,)),
            dma((3, 4)), dma((3, 4)),
            dma((3, 4)), dma((3, 4)),
        ],
        compiler_params=pltpu.CompilerParams(
            collective_id=0, has_side_effects=True, vmem_limit_bytes=60 * 2**20
        ),
    )(chosen, slot_weight, tokens, out_grad, w_gate, w_up, w_down)


def finish_kernel(pick, back, fin_g, fin_u, fin_d, token_grad, grad_gate, grad_up, grad_down):
    for n in range(4):
        part = pl.ds(128 * n, 128)
        token_grad[part, :] = dot(pick[:, part], back[...], TN).astype(BF)
    for j in range(4):
        grad_gate[0, :, QUARTER * j : QUARTER * (j + 1)] = fin_g[j, :, 0:QUARTER]
        grad_up[0, :, QUARTER * j : QUARTER * (j + 1)] = fin_u[j, :, 0:QUARTER]
    half = fin_d.shape[2]
    for y in range(2):
        grad_down[0, :, half * y : half * (y + 1)] = fin_d[y, 0:44, :]


def finish(pick, back, fin_g, fin_u, fin_d, hid):
    width = back.shape[1]
    vmem = pl.BlockSpec(memory_space=pltpu.VMEM)
    return pl.pallas_call(
        finish_kernel,
        out_shape=(
            jax.ShapeDtypeStruct((pick.shape[1], width), BF),
            jax.ShapeDtypeStruct((1, width // 32, hid), BF),
            jax.ShapeDtypeStruct((1, width // 32, hid), BF),
            jax.ShapeDtypeStruct((1, hid // 32, width), BF),
        ),
        in_specs=[vmem] * 5,
        out_specs=(vmem,) * 4,
        compiler_params=pltpu.CompilerParams(vmem_limit_bytes=60 * 2**20),
    )(pick, back, fin_g, fin_u, fin_d)


def local(tokens, out_grad, chosen, slot_weight, w_gate, w_up, w_down):
    pick, back, fin_g, fin_u, fin_d = main_pass(
        chosen, slot_weight, tokens, out_grad, w_gate, w_up, w_down
    )
    return finish(pick, back, fin_g, fin_u, fin_d, w_gate.shape[2])


def solution(mesh):
    return jax.shard_map(
        local,
        mesh=mesh,
        in_specs=(
            P(("dp", "expert"), None),
            P(("dp", "expert"), None),
            P(),
            P("expert", None),
            P("expert", None, None),
            P("expert", None, None),
            P("expert", None, None),
        ),
        out_specs=(
            P(("dp", "expert"), None),
            P("expert", "dp", None),
            P("expert", "dp", None),
            P("expert", "dp", None),
        ),
        check_vma=False,
    )
```

time: 494 us -> 63.1 us (0.13)
  blocking collectives: 256 us -> 0 us
  waiting for transfers between devices: 137 us -> 0 us
  Pallas kernels: 0 us -> 61.7 us
  matrix products: 34.4 us -> 0 us
  starting transfers between devices: 21.5 us -> 0 us
  other arithmetic: 18.7 us -> 0 us
  between operations: 14.9 us -> 0.64 us
  local copies, waits for them, and re-layouts: 9.59 us -> 0 us
    unnamed x1 -> x0, blocking collectives: 256 us -> none
    reduce_scatter x2 -> x0, waiting for transfers between devices: 131 us -> none  [the longest x1 131 us: local(): lax.psum_scatter(part_up.astype(jnp.bfloat16), 'dp', scatter_dimension=0,...]
    pallas_call x0 -> x2, Pallas kernels: none -> 61.7 us  [the longest x1 58.3 us: main_pass(): pl.pallas_call(main_kernel, out_shape=(jax.ShapeDtypeStruct((SLOTS, token...]
    dot_general x8 -> x0, matrix products: 34.4 us -> none  [the longest x3 12.6 us: contract_rows(): lax.dot_general(left_rows, right_rows, (((0,), (0,)), ((), ())), preferre...]
    all_to_all x3 -> x0, starting transfers between devices: 12.6 us -> none  [the longest x1 4.66 us: local(): lax.all_to_all(send_back.astype(jnp.bfloat16), 'expert', split_axis=0, co...]
    unnamed x3 -> x0, starting transfers between devices: 8.76 us -> none
    all_to_all x3 -> x0, waiting for transfers between devices: 6.42 us -> none  [the longest x1 6.39 us: local(): lax.all_to_all(send_tokens, 'expert', split_axis=0, concat_axis=0, tiled=...]
    gather x7 -> x0, local copies, waits for them, and re-layouts: 6.2 us -> none  [the longest x1 2.85 us: local(): out_grad[local_rows]]
  transfers between devices with their start and end apart: 8 -> 0, of which waited for: 2 -> 0; matrix products, arithmetic and copies ran while one was open for 60% -> 0% of each run, Pallas kernels for 0% -> 0%
where the time goes in v2:
time: 63.1 us; the launch traced here: 62.4 us
  Pallas kernels  61.7 us (98%)
  between operations  0.64 us (1%)
    pallas_call x1, Pallas kernels, main_pass(): pl.pallas_call(main_kernel, out_shape=(jax.ShapeDtypeStruct((SLOTS, token...  58.3 us
    pallas_call x1, Pallas kernels, finish(): pl.pallas_call(finish_kernel, out_shape=(jax.ShapeDtypeStruct((pick.shape...  3.38 us

profile of v2, /device:TPU:0, one launch (start us, length us, event | category | flops | bytes accessed | tf_op | source)
XLA Modules:
  0.0 62.4 jit_solution(15161398493705778118)
XLA Ops:
  0.6 58.3 %shard_map.102 = (bf16[64,512]{1,0:T(8,128)(2,1)}, bf16[64,2048]{1,0:T(8,128)(2,1)}, bf16[4,64,384]{2,1,0:T(8,128)(2,1)}, bf16[4,64,384]{2,1,0:T(8,128)(2,1)}, bf16[2,48,1024]{2,1,0:T(8,128)(2,1)}) custom-call(s32[4,1024]{1,0:T(4,128)} %chosen.1, f32[1,1024]{1,0:T(1,128)} %slot_weight.1, bf16[512,2048]{1,0:T(8,128)(2,1)} %tokens.1, ...), custom_call_target="tpu_custom_call" | custom-call | tf_op jit(solution)/shard_map/pallas_call | solution.py:340
  59.0 3.4 %shard_map.103 = (bf16[512,2048]{1,0:T(8,128)(2,1)}, bf16[1,64,1408]{2,1,0:T(8,128)(2,1)}, bf16[1,64,1408]{2,1,0:T(8,128)(2,1)}, bf16[1,44,2048]{2,1,0:T(8,128)(2,1)}) custom-call(bf16[64,512]{1,0:T(8,128)(2,1)} %get-tuple-element.9.pick, bf16[64,2048]{1,0:T(8,128)(2,1)} %get-tuple-element.10.back, bf16[4,64,384]{2,1,0:T(8,128)(2,1)} %get-tuple-element.11.fin_g, ...), custom_call_target="tpu_custom_call" | custom-call | tf_op jit(solution)/shard_map/pallas_call | solution.py:396

commit v3 on v2

v3 whole, which is shorter than its diff:
```python
import jax
import jax.numpy as jnp
from jax import lax
from jax.experimental import pallas as pl
from jax.experimental.pallas import tpu as pltpu
from jax.sharding import PartitionSpec as P

MESH = pl.DeviceIdType.MESH
BF = jnp.bfloat16
F32 = jnp.float32
MOST = 16
SLOTS = 64
QUARTER = 352
QPAD = 384
NN = (((1,), (0,)), ((), ()))
NT = (((1,), (1,)), ((), ()))
TN = (((0,), (0,)), ((), ()))


def dot(lhs, rhs, dims):
    return lax.dot_general(lhs, rhs, dims, preferred_element_type=F32)


def indicator(cond):
    return jnp.where(cond, 1.0, 0.0).astype(BF)


def route(me, dp, near, chosen, slot_weight, pick, weight):
    slots = chosen.shape[1]
    row = lax.broadcasted_iota(jnp.int32, (16, slots), 0)
    low_iota = lax.broadcasted_iota(jnp.int32, (128, slots), 0)
    lists = chosen[...]
    counts = jnp.zeros((16, 128), F32)
    value = slot_weight[...]
    part_a = value.astype(BF).astype(F32)
    part_b = (value - part_a).astype(BF).astype(F32)
    part_c = value - part_a - part_b
    for f in range(4):
        entries = lists[f : f + 1, :]
        low = indicator(low_iota == (entries & 127))
        tile = entries >> 7
        high = tile - (dp * 4 + me) * 4
        n = (f + 4 - me) % 4
        high = jnp.where((high >= 0) & (high < 4), high + 4 * n, -1)
        counts = counts + dot(indicator(row == high), low, NT)
        if f == 0:
            mine, mine_low = tile, low
        else:
            is_mine = me == f
            mine = jnp.where(is_mine, tile, mine)
            mine_low = jnp.where(is_mine, low, mine_low)
    wanted = 4 * ((me + 4 - (row >> 2)) & 3) + (row & 3)
    stacked = []
    for part in (jnp.ones_like(value), part_a, part_b, part_c):
        for group in (dp, near):
            stacked.append(jnp.where(wanted == mine - group * 16, part, 0.0).astype(BF))
    found = dot(jnp.concatenate(stacked, axis=0), mine_low, NT)
    weight_map = found[32:64] + found[64:96] + found[96:128]

    both = jnp.concatenate([counts, found[0:32]], axis=0)
    upper = indicator(
        lax.broadcasted_iota(jnp.int32, (128, 128), 0) <= lax.broadcasted_iota(jnp.int32, (128, 128), 1)
    )
    running = dot(both.astype(BF), upper, NN)
    totals = dot(both.astype(BF), jnp.ones((128, 128), BF), NN)
    left = lax.broadcasted_iota(jnp.int32, (48, 48), 0)
    right = lax.broadcasted_iota(jnp.int32, (48, 48), 1)
    before = indicator(((left >> 2) == (right >> 2)) & (right < left))
    rank = running + dot(before, totals.astype(BF), NN) - 1.0
    rank = jnp.where(both > 0.5, rank, -1.0)
    place = lax.broadcasted_iota(jnp.int32, (MOST, 512), 0).astype(F32)

    def line(values, first):
        return jnp.concatenate([values[first + h : first + h + 1, :] for h in range(4)], axis=1)

    for n in range(4):
        pick[16 * n : 16 * n + 16, :] = indicator(place == line(rank, 4 * n))
    for n in range(8):
        chosen_here = jnp.where(place == line(rank, 16 + 4 * n), line(weight_map, 4 * n), 0.0)
        weight[16 * n : 16 * n + 16, :] = jnp.broadcast_to(
            jnp.sum(chosen_here, axis=1, keepdims=True), (MOST, 128)
        )


def main_kernel(chosen_in, slot_weight_in, tokens, out_grad, w_gate, w_up, w_down,
                token_grad, grad_gate, grad_up, grad_down,
                chosen, slot_weight, pick, tok_buf, grad_buf, weight, rows_in, grads_in, wg, wu, wd,
                rows, raw, gout, rx, rg, rh, rgu, hq, gq, ggp, gup, slot_send, back, part_d, got_d,
                part_gu, got_gu, out_d, out_gu, land_d, land_gu,
                load_sem, w_sem, disp_s, disp_r, early_s, early_r, late_s, late_r,
                ret_s, ret_r, sum_s, sum_r, put_s, put_r):
    dp = lax.axis_index("dp")
    me = lax.axis_index("expert")
    yl = dp % 2
    core = me % 2
    along_x = (dp // 2) % 4
    along_z = dp // 8
    a = along_x + core * (along_z - along_x)
    b = along_z + core * (along_x - along_z)

    def at_dp(a_at, b_at, y_at):
        return a_at * (2 + 6 * core) + b_at * (8 - 6 * core) + y_at

    ring_a = [(at_dp((a + n) % 4, b, yl), me) for n in range(4)]
    ring_b = [(at_dp(a, (b + n) % 4, yl), me) for n in range(4)]
    across = (at_dp(a, b, 1 - yl), me)
    started = []

    def send(src, dst, send_sem, recv_sem, target):
        copy = pltpu.make_async_remote_copy(
            src_ref=src, dst_ref=dst, send_sem=send_sem, recv_sem=recv_sem,
            device_id=target, device_id_type=MESH,
        )
        copy.start()
        started.append(copy)
        return copy

    barrier = pltpu.get_barrier_semaphore()
    near = dp + 1 - 2 * yl
    group = [(dp, (me + n) % 4) for n in range(4)]
    near_group = [(near, (me + n) % 4) for n in range(4)]
    friends = group[1:] + near_group + ring_a[1:] + ring_b[1:]
    for friend in friends:
        pl.semaphore_signal(barrier, inc=1, device_id=friend, device_id_type=MESH)

    loads = [
        pltpu.make_async_copy(src, dst, load_sem.at[n])
        for n, (src, dst) in enumerate(
            ((chosen_in, chosen), (slot_weight_in, slot_weight), (tokens, tok_buf), (out_grad, grad_buf))
        )
    ]
    weights = []
    for n, (src, dst) in enumerate(((w_gate, wg), (w_up, wu), (w_down, wd))):
        middle = dst.shape[0] // 2
        for h in range(2):
            part = pl.ds(h * middle, middle)
            weights.append(pltpu.make_async_copy(src.at[0, part], dst.at[part], w_sem.at[2 * n + h]))
    for copy in loads:
        copy.start()
    for copy in loads[0:2]:
        copy.wait()
    route(me, dp, near, chosen, slot_weight, pick, weight)
    for copy in loads[2:4]:
        copy.wait()
    for copy in weights:
        copy.start()
    rows_in[...] = dot(pick[...], tok_buf[...], NN).astype(BF)
    pl.semaphore_wait(barrier, len(friends))

    block = lambda n: pl.ds(MOST * n, MOST)

    def dispatch(which, g, src, dst):
        return [
            send(src.at[block(n)], dst.at[block(4 * g + n)], disp_s.at[which, 4 * g + n],
                 disp_r.at[which, 4 * g + n], (near_group if g else group)[n])
            for n in (2, 3, 1, 0) if g or n
        ]

    row_copies = [dispatch(0, 0, rows_in, rows)]
    rows[0:MOST, :] = rows_in[0:MOST, :]
    grads_in[...] = dot(pick[...], grad_buf[...], NN).astype(BF)
    grad_copies = [dispatch(1, 0, grads_in, raw)]
    raw[0:MOST, :] = grads_in[0:MOST, :]

    half = rows.shape[1] // 2
    mine = pl.ds(pl.multiple_of(yl * half, half), half)
    slot = lambda d, g: pl.ds(2 * SLOTS * d + SLOTS * g, SLOTS)
    gap = jnp.zeros((SLOTS, 4), BF)
    blank = jnp.zeros((SLOTS, QPAD - QUARTER), BF)
    early_x, early_g, late_h, late_gu = [], [], [], []

    def early_sends(which, g, src, dst):
        return [
            send(src, dst.at[slot(n, g)], early_s.at[which, 4 * g + n], early_r.at[which, 4 * g + n], ring_a[n])
            for n in (2, 1, 3)
        ]

    def late_sends(which, g, src, dst):
        here = pl.ds(SLOTS * g, SLOTS)
        dst[here, :] = src[a, here, :]
        return [
            send(src.at[(a + n) % 4, here], dst.at[slot(n, g)], late_s.at[which, 4 * g + n],
                 late_r.at[which, 4 * g + n], ring_a[n])
            for n in (2, 1, 3)
        ]

    for g in range(2):
        here = pl.ds(SLOTS * g, SLOTS)
        for copy in row_copies[g]:
            copy.wait_recv()
        if g == 0:
            row_copies.append(dispatch(0, 1, rows_in, rows))
        for which in range(4):
            @pl.when(2 * core + yl == which)
            def _():
                order = [u if which < 2 else 4 * (u % 4) + u // 4 for u in range(16)]
                first = 64 * (which % 2)
                rx[here, :] = jnp.concatenate(
                    [rows[here, 128 * u + first : 128 * u + first + 64] for u in order], axis=1
                )
        early_x += early_sends(0, g, rx.at[here], rx)

        if g == 0:
            for copy in weights[0:4]:
                copy.wait()
        gate_pre = dot(rows[here, :], wg[...], NN)
        up_pre = dot(rows[here, :], wu[...], NN)
        sig = 1.0 / (1.0 + jnp.exp(-gate_pre))
        activated = gate_pre * sig
        ggp[here, :] = (activated * up_pre).astype(BF)
        for which in range(2):
            @pl.when(core == which)
            def _():
                for j in range(4):
                    pieces = []
                    for v in range(8):
                        owner = (v // 2) * 8 + 2 * j + v % 2 if which == 0 else 8 * j + v
                        pieces += [ggp[here, 44 * owner : 44 * owner + 44], gap]
                    hq[j, here, :] = jnp.concatenate(pieces, axis=1)
        late_h += late_sends(0, g, hq, rh)

        for copy in grad_copies[g]:
            copy.wait_recv()
        if g == 0:
            grad_copies.append(dispatch(1, 1, grads_in, raw))
        gout[here, :] = (weight[here, 0:1] * raw[here, :].astype(F32)).astype(BF)
        rg[here, :] = gout[here, mine]
        early_g += early_sends(1, g, rg.at[here], rg)
        if g == 0:
            for copy in weights[4:6]:
                copy.wait()
        grad_hidden = dot(gout[here, :], wd[...], NT)
        gup[here, :] = (grad_hidden * activated).astype(BF)
        ggp[here, :] = (grad_hidden * up_pre * (sig * (1.0 + gate_pre * (1.0 - sig)))).astype(BF)
        for j in range(4):
            columns = slice(QUARTER * j, QUARTER * (j + 1))
            gq[j, here, :] = jnp.concatenate([gup[here, columns], blank, ggp[here, columns], blank], axis=1)
        late_gu += late_sends(1, g, gq, rgu)

    chunk = half // 4
    sums = [[], [], []]
    for copy in early_g + late_h:
        copy.wait_recv()
    part_d[...] = dot(rh[...], rg[...], TN).astype(BF)
    rows_d = QPAD // 4
    for n in (2, 1, 3):
        sums[0].append(send(
            part_d.at[pl.ds(pl.multiple_of((b + n) % 4 * rows_d, rows_d), rows_d)], got_d.at[n],
            sum_s.at[0, n], sum_r.at[0, n], ring_b[n],
        ))
    for copy in early_x + late_gu:
        copy.wait_recv()
    for part in (1, 2):
        for n in (2, 1, 3, 0):
            columns = pl.ds(pl.multiple_of((b + n) % 4 * chunk, chunk), chunk)
            part_gu[part - 1, n] = dot(rx[:, columns], rgu[:, QPAD * (part - 1) : QPAD * part], TN).astype(BF)
            if n:
                sums[part].append(send(
                    part_gu.at[part - 1, n], got_gu.at[part - 1, n],
                    sum_s.at[part, n], sum_r.at[part, n], ring_b[n],
                ))

    slot_grad = dot(ggp[0:SLOTS, :], wg[...], NT) + dot(gup[0:SLOTS, :], wu[...], NT)
    slot_send[...] = slot_grad.astype(BF)
    returns = [
        send(slot_send.at[block(n)], back.at[block(n)], ret_s.at[n], ret_r.at[n], (dp, (me + 4 - n) % 4))
        for n in (2, 1, 3)
    ]
    back[0:MOST, :] = slot_send[0:MOST, :]

    scale = 1.0 / 32
    for copy in sums[0]:
        copy.wait_recv()
    total = part_d[pl.ds(pl.multiple_of(b * rows_d, rows_d), rows_d), :].astype(F32)
    for n in range(1, 4):
        total = total + got_d[n].astype(F32)
    out_d[...] = (total * scale).astype(BF).reshape(out_d.shape)
    put_d = send(out_d.at[1 - yl], land_d.at[yl], put_s.at[0, 0], put_r.at[0, 0], across)
    land_d[yl] = out_d[yl]
    for copy in returns:
        copy.wait_recv()
    for n in range(4):
        part = pl.ds(128 * n, 128)
        token_grad[part, :] = dot(pick[:, part], back[...], TN).astype(BF)
    for part in (1, 2):
        for copy in sums[part]:
            copy.wait_recv()
        total = part_gu[part - 1, 0].astype(F32)
        for n in range(1, 4):
            total = total + got_gu[part - 1, n].astype(F32)
        out_gu[part - 1] = (total * scale).astype(BF).reshape(out_gu.shape[1:])
        for n in (2, 1, 3):
            send(out_gu.at[part - 1, (a + n) % 4], land_gu.at[part - 1, a], put_s.at[part, n],
                 put_r.at[part, n], ring_a[n])
        land_gu[part - 1, a] = out_gu[part - 1, a]

    pltpu.make_async_copy(land_d.at[1 - yl], land_d.at[1 - yl], put_r.at[0, 0]).wait()
    for y in range(2):
        grad_down[0, :, half * y : half * (y + 1)] = land_d[y, 0:44, :]
    for part, dst in ((1, grad_up), (2, grad_gate)):
        for n in (1, 2, 3):
            there = land_gu.at[part - 1, (a + 4 - n) % 4]
            pltpu.make_async_copy(there, there, put_r.at[part, n]).wait()
        for j in range(4):
            dst[0, :, QUARTER * j : QUARTER * (j + 1)] = land_gu[part - 1, j, :, 0:QUARTER]
    for copy in started:
        copy.wait_send()


def main_pass(chosen, slot_weight, tokens, out_grad, w_gate, w_up, w_down):
    width = tokens.shape[1]
    hid = w_gate.shape[2]
    half = width // 2
    chunk = half // 4
    vmem = pl.BlockSpec(memory_space=pltpu.VMEM)
    hbm = pl.BlockSpec(memory_space=pl.ANY)
    dma = pltpu.SemaphoreType.DMA

    def buf(*shape):
        return pltpu.VMEM(shape, BF)

    return pl.pallas_call(
        main_kernel,
        out_shape=(
            pltpu.VMEM(tokens.shape, BF),
            pltpu.VMEM((1, width // 32, hid), BF),
            pltpu.VMEM((1, width // 32, hid), BF),
            pltpu.VMEM((1, hid // 32, width), BF),
        ),
        in_specs=[hbm] * 7,
        out_specs=(vmem,) * 4,
        scratch_shapes=[
            pltpu.VMEM(chosen.shape, jnp.int32), pltpu.VMEM(slot_weight.shape, F32),
            buf(SLOTS, tokens.shape[0]),
            buf(*tokens.shape), buf(*tokens.shape),
            pltpu.VMEM((2 * SLOTS, 128), F32),
            buf(SLOTS, width), buf(SLOTS, width),
            buf(width, hid), buf(width, hid), buf(hid, width),
            buf(2 * SLOTS, width), buf(2 * SLOTS, width), buf(2 * SLOTS, width),
            buf(8 * SLOTS, half), buf(8 * SLOTS, half),
            buf(8 * SLOTS, QPAD), buf(8 * SLOTS, 2 * QPAD),
            buf(4, 2 * SLOTS, QPAD), buf(4, 2 * SLOTS, 2 * QPAD),
            buf(2 * SLOTS, hid), buf(2 * SLOTS, hid),
            buf(SLOTS, width), buf(SLOTS, width),
            buf(QPAD, half), buf(4, QPAD // 4, half),
            buf(2, 4, chunk, QPAD), buf(2, 4, chunk, QPAD),
            buf(2, 48, half), buf(2, 4, 64, QPAD),
            buf(2, 48, half), buf(2, 4, 64, QPAD),
            dma((4,)), dma((6,)),
            dma((2, 8)), dma((2, 8)),
            dma((2, 8)), dma((2, 8)),
            dma((2, 8)), dma((2, 8)),
            dma((4,)), dma((4,)),
            dma((3, 4)), dma((3, 4)),
            dma((3, 4)), dma((3, 4)),
        ],
        compiler_params=pltpu.CompilerParams(
            collective_id=0, has_side_effects=True, vmem_limit_bytes=56 * 2**20
        ),
    )(chosen, slot_weight, tokens, out_grad, w_gate, w_up, w_down)


def store_kernel(*refs):
    sources, results, sems = refs[0:4], refs[4:8], refs[8]
    copies = [pltpu.make_async_copy(sources[n], results[n], sems.at[n]) for n in range(4)]
    for copy in copies:
        copy.start()
    for copy in copies:
        copy.wait()


def local(tokens, out_grad, chosen, slot_weight, w_gate, w_up, w_down):
    results = main_pass(chosen, slot_weight, tokens, out_grad, w_gate, w_up, w_down)
    return pl.pallas_call(
        store_kernel,
        out_shape=tuple(jax.ShapeDtypeStruct(value.shape, value.dtype) for value in results),
        in_specs=[pl.BlockSpec(memory_space=pltpu.VMEM)] * 4,
        out_specs=(pl.BlockSpec(memory_space=pl.ANY),) * 4,
        scratch_shapes=[pltpu.SemaphoreType.DMA((4,))],
        compiler_params=pltpu.CompilerParams(vmem_limit_bytes=4 * 2**20),
    )(*results)


def solution(mesh):
    return jax.shard_map(
        local,
        mesh=mesh,
        in_specs=(
            P(("dp", "expert"), None),
            P(("dp", "expert"), None),
            P(),
            P("expert", None),
            P("expert", None, None),
            P("expert", None, None),
            P("expert", None, None),
        ),
        out_specs=(
            P(("dp", "expert"), None),
            P("expert", "dp", None),
            P("expert", "dp", None),
            P("expert", "dp", None),
        ),
        check_vma=False,
    )
```

time: 63.1 us -> 56.4 us (0.89)
  Pallas kernels: 61.7 us -> 54.8 us
    pallas_call x2, Pallas kernels: 61.7 us -> 54.8 us  [the longest x1 53.3 us: main_pass(): pl.pallas_call(main_kernel, out_shape=(pltpu.VMEM(tokens.shape, BF), pltp...]
where the time goes in v3:
time: 56.4 us; the launch traced here: 55.6 us
  Pallas kernels  54.8 us (97%)
  between operations  0.8 us (1%)
    pallas_call x1, Pallas kernels, main_pass(): pl.pallas_call(main_kernel, out_shape=(pltpu.VMEM(tokens.shape, BF), pltp...  53.3 us
    pallas_call x1, Pallas kernels, local(): pl.pallas_call(store_kernel, out_shape=tuple((jax.ShapeDtypeStruct(value....  1.52 us

profile of v3, /device:TPU:0, one launch (start us, length us, event | category | flops | bytes accessed | tf_op | source)
XLA Modules:
  0.0 55.6 jit_solution(2224490676659249752)
XLA Ops:
  0.6 53.3 %shard_map.102 = (bf16[512,2048]{1,0:T(8,128)(2,1)S(1)}, bf16[1,64,1408]{2,1,0:T(8,128)(2,1)S(1)}, bf16[1,64,1408]{2,1,0:T(8,128)(2,1)S(1)}, bf16[1,44,2048]{2,1,0:T(8,128)(2,1)S(1)}) custom-call(s32[4,1024]{1,0:T(4,128)} %chosen_in.1, f32[1,1024]{1,0:T(1,128)} %slot_weight_in.1, bf16[512,2048]{1,0:T(8,128)(2,1)} %tokens.1, bf16[512,2048]{1,0:T(8,128)(2,1)} %out_grad.1, ...), custom_call_target="tpu_custom_call" | custom-call | tf_op jit(solution)/shard_map/pallas_call | solution.py:322
  54.0 1.5 %shard_map.103 = (bf16[512,2048]{1,0:T(8,128)(2,1)}, bf16[1,64,1408]{2,1,0:T(8,128)(2,1)}, bf16[1,64,1408]{2,1,0:T(8,128)(2,1)}, bf16[1,44,2048]{2,1,0:T(8,128)(2,1)}) custom-call(bf16[512,2048]{1,0:T(8,128)(2,1)S(1)} %get-tuple-element.8.refs_0_, bf16[1,64,1408]{2,1,0:T(8,128)(2,1)S(1)} %get-tuple-element.9.refs_1_, ...), custom_call_target="tpu_custom_call" | custom-call | tf_op jit(solution)/shard_map/pallas_call | solution.py:374

commit v4 on v3

--- a/solution.py
+++ b/solution.py
@@ -25,58 +25,67 @@
     return jnp.where(cond, 1.0, 0.0).astype(BF)
 
 
-def route(me, dp, near, chosen, slot_weight, pick, weight):
-    slots = chosen.shape[1]
-    row = lax.broadcasted_iota(jnp.int32, (16, slots), 0)
-    low_iota = lax.broadcasted_iota(jnp.int32, (128, slots), 0)
+def one_hot(entries, rows, tile):
+    low = lax.broadcasted_iota(jnp.int32, (128, entries.shape[1]), 0) == (entries & 127)
+    return rows == tile, indicator(low)
+
+
+def ranks(counts):
+    size = counts.shape[0]
+    upper = indicator(
+        lax.broadcasted_iota(jnp.int32, (128, 128), 0) <= lax.broadcasted_iota(jnp.int32, (128, 128), 1)
+    )
+    running = dot(counts.astype(BF), upper, NN)
+    totals = dot(counts.astype(BF), jnp.ones((128, 128), BF), NN)
+    left = lax.broadcasted_iota(jnp.int32, (size, size), 0)
+    right = lax.broadcasted_iota(jnp.int32, (size, size), 1)
+    before = indicator(((left >> 2) == (right >> 2)) & (right < left))
+    rank = running + dot(before, totals.astype(BF), NN) - 1.0
+    return jnp.where(counts > 0.5, rank, -1.0)
+
+
+def line(values, n):
+    return jnp.concatenate([values[4 * n + h : 4 * n + h + 1, :] for h in range(4)], axis=1)
+
+
+def route_picks(me, dp, chosen, pick):
+    row = lax.broadcasted_iota(jnp.int32, (16, chosen.shape[1]), 0)
     lists = chosen[...]
     counts = jnp.zeros((16, 128), F32)
+    for f in range(4):
+        entries = lists[f : f + 1, :]
+        high = (entries >> 7) - (dp * 4 + me) * 4
+        high = jnp.where((high >= 0) & (high < 4), high + 4 * ((f + 4 - me) % 4), -1)
+        tile, low = one_hot(entries, row, high)
+        counts = counts + dot(indicator(tile), low, NT)
+    rank = ranks(counts)
+    place = lax.broadcasted_iota(jnp.int32, (MOST, 512), 0).astype(F32)
+    for n in range(4):
+        pick[16 * n : 16 * n + 16, :] = indicator(place == line(rank, n))
+
+
+def route_weights(me, dp, near, chosen, slot_weight, weight):
+    lists = chosen[...]
+    entries = lists[0:1, :]
+    for f in range(1, 4):
+        entries = jnp.where(me == f, lists[f : f + 1, :], entries)
+    row = lax.broadcasted_iota(jnp.int32, (16, chosen.shape[1]), 0)
+    wanted = 4 * ((me + 4 - (row >> 2)) & 3) + (row & 3)
     value = slot_weight[...]
     part_a = value.astype(BF).astype(F32)
     part_b = (value - part_a).astype(BF).astype(F32)
     part_c = value - part_a - part_b
-    for f in range(4):
-        entries = lists[f : f + 1, :]
-        low = indicator(low_iota == (entries & 127))
-        tile = entries >> 7
-        high = tile - (dp * 4 + me) * 4
-        n = (f + 4 - me) % 4
-        high = jnp.where((high >= 0) & (high < 4), high + 4 * n, -1)
-        counts = counts + dot(indicator(row == high), low, NT)
-        if f == 0:
-            mine, mine_low = tile, low
-        else:
-            is_mine = me == f
-            mine = jnp.where(is_mine, tile, mine)
-            mine_low = jnp.where(is_mine, low, mine_low)
-    wanted = 4 * ((me + 4 - (row >> 2)) & 3) + (row & 3)
     stacked = []
     for part in (jnp.ones_like(value), part_a, part_b, part_c):
         for group in (dp, near):
-            stacked.append(jnp.where(wanted == mine - group * 16, part, 0.0).astype(BF))
-    found = dot(jnp.concatenate(stacked, axis=0), mine_low, NT)
+            hit, low = one_hot(entries, wanted, (entries >> 7) - group * 16)
+            stacked.append(jnp.where(hit, part, 0.0).astype(BF))
+    found = dot(jnp.concatenate(stacked, axis=0), low, NT)
     weight_map = found[32:64] + found[64:96] + found[96:128]
-
-    both = jnp.concatenate([counts, found[0:32]], axis=0)
-    upper = indicator(
-        lax.broadcasted_iota(jnp.int32, (128, 128), 0) <= lax.broadcasted_iota(jnp.int32, (128, 128), 1)
-    )
-    running = dot(both.astype(BF), upper, NN)
-    totals = dot(both.astype(BF), jnp.ones((128, 128), BF), NN)
-    left = lax.broadcasted_iota(jnp.int32, (48, 48), 0)
-    right = lax.broadcasted_iota(jnp.int32, (48, 48), 1)
-    before = indicator(((left >> 2) == (right >> 2)) & (right < left))
-    rank = running + dot(before, totals.astype(BF), NN) - 1.0
-    rank = jnp.where(both > 0.5, rank, -1.0)
+    rank = ranks(found[0:32])
     place = lax.broadcasted_iota(jnp.int32, (MOST, 512), 0).astype(F32)
-
-    def line(values, first):
-        return jnp.concatenate([values[first + h : first + h + 1, :] for h in range(4)], axis=1)
-
-    for n in range(4):
-        pick[16 * n : 16 * n + 16, :] = indicator(place == line(rank, 4 * n))
     for n in range(8):
-        chosen_here = jnp.where(place == line(rank, 16 + 4 * n), line(weight_map, 4 * n), 0.0)
+        chosen_here = jnp.where(place == line(rank, n), line(weight_map, n), 0.0)
         weight[16 * n : 16 * n + 16, :] = jnp.broadcast_to(
             jnp.sum(chosen_here, axis=1, keepdims=True), (MOST, 128)
         )
@@ -85,8 +94,8 @@
 def main_kernel(chosen_in, slot_weight_in, tokens, out_grad, w_gate, w_up, w_down,
                 token_grad, grad_gate, grad_up, grad_down,
                 chosen, slot_weight, pick, tok_buf, grad_buf, weight, rows_in, grads_in, wg, wu, wd,
-                rows, raw, gout, rx, rg, rh, rgu, hq, gq, ggp, gup, slot_send, back, part_d, got_d,
-                part_gu, got_gu, out_d, out_gu, land_d, land_gu,
+                rows, raw, gout, rx, rg, rh, rgu, hq, gq, ggp, gup, slot_send, back, part_d, via_d, got_d,
+                part_gu, via_gu, got_gu, out_d, out_gu, land_d, land_gu,
                 load_sem, w_sem, disp_s, disp_r, early_s, early_r, late_s, late_r,
                 ret_s, ret_r, sum_s, sum_r, put_s, put_r):
     dp = lax.axis_index("dp")
@@ -137,13 +146,9 @@
             weights.append(pltpu.make_async_copy(src.at[0, part], dst.at[part], w_sem.at[2 * n + h]))
     for copy in loads:
         copy.start()
-    for copy in loads[0:2]:
-        copy.wait()
-    route(me, dp, near, chosen, slot_weight, pick, weight)
-    for copy in loads[2:4]:
-        copy.wait()
-    for copy in weights:
-        copy.start()
+    loads[0].wait()
+    route_picks(me, dp, chosen, pick)
+    loads[2].wait()
     rows_in[...] = dot(pick[...], tok_buf[...], NN).astype(BF)
     pl.semaphore_wait(barrier, len(friends))
 
@@ -158,9 +163,14 @@
 
     row_copies = [dispatch(0, 0, rows_in, rows)]
     rows[0:MOST, :] = rows_in[0:MOST, :]
+    loads[3].wait()
+    for copy in weights:
+        copy.start()
     grads_in[...] = dot(pick[...], grad_buf[...], NN).astype(BF)
     grad_copies = [dispatch(1, 0, grads_in, raw)]
     raw[0:MOST, :] = grads_in[0:MOST, :]
+    loads[1].wait()
+    route_weights(me, dp, near, chosen, slot_weight, weight)
 
     half = rows.shape[1] // 2
     mine = pl.ds(pl.multiple_of(yl * half, half), half)
@@ -238,27 +248,61 @@
         late_gu += late_sends(1, g, gq, rgu)
 
     chunk = half // 4
-    sums = [[], [], []]
+    rows_d = QPAD // 4
+
+    def far_sends(part, first, second, dst):
+        return [
+            send(first, dst.at[0], sum_s.at[part, 0], sum_r.at[part, 0], ring_b[1]),
+            send(second, dst.at[1], sum_s.at[part, 2], sum_r.at[part, 2], ring_b[3]),
+        ]
+
+    def near_sends(part, after, before, dst):
+        return [
+            send(after, dst.at[0], sum_s.at[part, 1], sum_r.at[part, 1], ring_b[1]),
+            send(before, dst.at[1], sum_s.at[part, 3], sum_r.at[part, 3], ring_b[3]),
+        ]
+
+    def tile_gu(part, n):
+        columns = pl.ds(pl.multiple_of((b + n) % 4 * chunk, chunk), chunk)
+        part_gu[part - 1, n] = dot(rx[:, columns], rgu[:, QPAD * (part - 1) : QPAD * part], TN).astype(BF)
+
+    def rows_at(n, h):
+        step = rows_d // 2
+        return pl.ds(pl.multiple_of((b + n) % 4 * rows_d, rows_d) + h * step, step)
+
     for copy in early_g + late_h:
         copy.wait_recv()
     part_d[...] = dot(rh[...], rg[...], TN).astype(BF)
-    rows_d = QPAD // 4
-    for n in (2, 1, 3):
-        sums[0].append(send(
-            part_d.at[pl.ds(pl.multiple_of((b + n) % 4 * rows_d, rows_d), rows_d)], got_d.at[n],
-            sum_s.at[0, n], sum_r.at[0, n], ring_b[n],
-        ))
+    relays = [far_sends(0, part_d.at[rows_at(2, 0)], part_d.at[rows_at(2, 1)], via_d)]
     for copy in early_x + late_gu:
         copy.wait_recv()
+    middle = chunk // 2
     for part in (1, 2):
-        for n in (2, 1, 3, 0):
-            columns = pl.ds(pl.multiple_of((b + n) % 4 * chunk, chunk), chunk)
-            part_gu[part - 1, n] = dot(rx[:, columns], rgu[:, QPAD * (part - 1) : QPAD * part], TN).astype(BF)
-            if n:
-                sums[part].append(send(
-                    part_gu.at[part - 1, n], got_gu.at[part - 1, n],
-                    sum_s.at[part, n], sum_r.at[part, n], ring_b[n],
-                ))
+        tile_gu(part, 2)
+        far = part_gu.at[part - 1, 2]
+        relays.append(far_sends(part, far.at[0:middle], far.at[middle:chunk], via_gu.at[part - 1]))
+    tile_gu(1, 1)
+    tile_gu(1, 3)
+    sums = []
+    for copy in relays[0]:
+        copy.wait_recv()
+    for n, h in ((1, 0), (3, 1)):
+        part_d[rows_at(n, h), :] = (part_d[rows_at(n, h), :].astype(F32) + via_d[h].astype(F32)).astype(BF)
+    whole = lambda n: pl.ds(pl.multiple_of((b + n) % 4 * rows_d, rows_d), rows_d)
+    sums.append(near_sends(0, part_d.at[whole(1)], part_d.at[whole(3)], got_d))
+    tile_gu(2, 1)
+    tile_gu(2, 3)
+    for part in (1, 2):
+        for copy in relays[part]:
+            copy.wait_recv()
+        for n, h in ((1, 0), (3, 1)):
+            rows_h = pl.ds(middle * h, middle)
+            part_gu[part - 1, n, rows_h, :] = (
+                part_gu[part - 1, n, rows_h, :].astype(F32) + via_gu[part - 1, h].astype(F32)
+            ).astype(BF)
+        sums.append(near_sends(part, part_gu.at[part - 1, 1], part_gu.at[part - 1, 3], got_gu.at[part - 1]))
+    tile_gu(1, 0)
+    tile_gu(2, 0)
 
     slot_grad = dot(ggp[0:SLOTS, :], wg[...], NT) + dot(gup[0:SLOTS, :], wu[...], NT)
     slot_send[...] = slot_grad.astype(BF)
@@ -272,21 +316,16 @@
     for copy in sums[0]:
         copy.wait_recv()
     total = part_d[pl.ds(pl.multiple_of(b * rows_d, rows_d), rows_d), :].astype(F32)
-    for n in range(1, 4):
+    for n in range(2):
         total = total + got_d[n].astype(F32)
     out_d[...] = (total * scale).astype(BF).reshape(out_d.shape)
     put_d = send(out_d.at[1 - yl], land_d.at[yl], put_s.at[0, 0], put_r.at[0, 0], across)
     land_d[yl] = out_d[yl]
-    for copy in returns:
-        copy.wait_recv()
-    for n in range(4):
-        part = pl.ds(128 * n, 128)
-        token_grad[part, :] = dot(pick[:, part], back[...], TN).astype(BF)
     for part in (1, 2):
         for copy in sums[part]:
             copy.wait_recv()
         total = part_gu[part - 1, 0].astype(F32)
-        for n in range(1, 4):
+        for n in range(2):
             total = total + got_gu[part - 1, n].astype(F32)
         out_gu[part - 1] = (total * scale).astype(BF).reshape(out_gu.shape[1:])
         for n in (2, 1, 3):
@@ -294,6 +333,13 @@
                  put_r.at[part, n], ring_a[n])
         land_gu[part - 1, a] = out_gu[part - 1, a]
 
+    for copy in started[:-7]:
+        copy.wait_send()
+    for copy in returns:
+        copy.wait_recv()
+    for n in range(4):
+        part = pl.ds(128 * n, 128)
+        token_grad[part, :] = dot(pick[:, part], back[...], TN).astype(BF)
     pltpu.make_async_copy(land_d.at[1 - yl], land_d.at[1 - yl], put_r.at[0, 0]).wait()
     for y in range(2):
         grad_down[0, :, half * y : half * (y + 1)] = land_d[y, 0:44, :]
@@ -303,7 +349,7 @@
             pltpu.make_async_copy(there, there, put_r.at[part, n]).wait()
         for j in range(4):
             dst[0, :, QUARTER * j : QUARTER * (j + 1)] = land_gu[part - 1, j, :, 0:QUARTER]
-    for copy in started:
+    for copy in started[-7:]:
         copy.wait_send()
 
 
@@ -342,8 +388,8 @@
             buf(4, 2 * SLOTS, QPAD), buf(4, 2 * SLOTS, 2 * QPAD),
             buf(2 * SLOTS, hid), buf(2 * SLOTS, hid),
             buf(SLOTS, width), buf(SLOTS, width),
-            buf(QPAD, half), buf(4, QPAD // 4, half),
-            buf(2, 4, chunk, QPAD), buf(2, 4, chunk, QPAD),
+            buf(QPAD, half), buf(2, QPAD // 8, half), buf(2, QPAD // 4, half),
+            buf(2, 4, chunk, QPAD), buf(2, 2, chunk // 2, QPAD), buf(2, 2, chunk, QPAD),
             buf(2, 48, half), buf(2, 4, 64, QPAD),
             buf(2, 48, half), buf(2, 4, 64, QPAD),
             dma((4,)), dma((6,)),

time: 56.4 us -> 53.9 us (0.956)
  Pallas kernels: 54.8 us -> 52.4 us
    pallas_call x1, Pallas kernels: 53.3 us -> 50.9 us  [main_pass(): pl.pallas_call(main_kernel, out_shape=(pltpu.VMEM(tokens.shape, BF), pltp...]
where the time goes in v4:
time: 53.9 us; the launch traced here: 53.2 us
  Pallas kernels  52.4 us (97%)
  between operations  0.8 us (1%)
    pallas_call x1, Pallas kernels, main_pass(): pl.pallas_call(main_kernel, out_shape=(pltpu.VMEM(tokens.shape, BF), pltp...  50.9 us
    pallas_call x1, Pallas kernels, local(): pl.pallas_call(store_kernel, out_shape=tuple((jax.ShapeDtypeStruct(value....  1.52 us

profile of v4, /device:TPU:0, one launch (start us, length us, event | category | flops | bytes accessed | tf_op | source)
XLA Modules:
  0.0 53.2 jit_solution(4710953418739830622)
XLA Ops:
  0.6 50.9 %shard_map.102 = (bf16[512,2048]{1,0:T(8,128)(2,1)S(1)}, bf16[1,64,1408]{2,1,0:T(8,128)(2,1)S(1)}, bf16[1,64,1408]{2,1,0:T(8,128)(2,1)S(1)}, bf16[1,44,2048]{2,1,0:T(8,128)(2,1)S(1)}) custom-call(s32[4,1024]{1,0:T(4,128)} %chosen_in.1, f32[1,1024]{1,0:T(1,128)} %slot_weight_in.1, bf16[512,2048]{1,0:T(8,128)(2,1)} %tokens.1, bf16[512,2048]{1,0:T(8,128)(2,1)} %out_grad.1, ...), custom_call_target="tpu_custom_call" | custom-call | tf_op jit(solution)/shard_map/pallas_call | solution.py:368
  51.5 1.5 %shard_map.103 = (bf16[512,2048]{1,0:T(8,128)(2,1)}, bf16[1,64,1408]{2,1,0:T(8,128)(2,1)}, bf16[1,64,1408]{2,1,0:T(8,128)(2,1)}, bf16[1,44,2048]{2,1,0:T(8,128)(2,1)}) custom-call(bf16[512,2048]{1,0:T(8,128)(2,1)S(1)} %get-tuple-element.8.refs_0_, bf16[1,64,1408]{2,1,0:T(8,128)(2,1)S(1)} %get-tuple-element.9.refs_1_, ...), custom_call_target="tpu_custom_call" | custom-call | tf_op jit(solution)/shard_map/pallas_call | solution.py:420

commit v5 on v4

--- a/solution.py
+++ b/solution.py
@@ -163,27 +163,40 @@
 
     row_copies = [dispatch(0, 0, rows_in, rows)]
     rows[0:MOST, :] = rows_in[0:MOST, :]
+    loads[1].wait()
+    route_weights(me, dp, near, chosen, slot_weight, weight)
     loads[3].wait()
     for copy in weights:
         copy.start()
     grads_in[...] = dot(pick[...], grad_buf[...], NN).astype(BF)
     grad_copies = [dispatch(1, 0, grads_in, raw)]
     raw[0:MOST, :] = grads_in[0:MOST, :]
-    loads[1].wait()
-    route_weights(me, dp, near, chosen, slot_weight, weight)
 
     half = rows.shape[1] // 2
     mine = pl.ds(pl.multiple_of(yl * half, half), half)
     slot = lambda d, g: pl.ds(2 * SLOTS * d + SLOTS * g, SLOTS)
     gap = jnp.zeros((SLOTS, 4), BF)
     blank = jnp.zeros((SLOTS, QPAD - QUARTER), BF)
-    early_x, early_g, late_h, late_gu = [], [], [], []
-
-    def early_sends(which, g, src, dst):
+    x_copies, g_copies, late_h, late_gu = [], [], [], []
+
+    def early_sends(which, g, src, dst, reach):
         return [
             send(src, dst.at[slot(n, g)], early_s.at[which, 4 * g + n], early_r.at[which, 4 * g + n], ring_a[n])
-            for n in (2, 1, 3)
+            for n in reach
         ]
+
+    def early_forward(which, g, copies, dst):
+        for copy in copies:
+            copy.wait_recv()
+        middle = SLOTS // 2
+        forwards = []
+        for h, n in ((0, 1), (1, 3)):
+            there = lambda d: pl.ds(2 * SLOTS * d + SLOTS * g + middle * h, middle)
+            forwards.append(send(
+                dst.at[there(n)], dst.at[there(2)], early_s.at[which, 4 * g + 2 * h],
+                early_r.at[which, 4 * g + 2 * h], ring_a[n],
+            ))
+        return forwards
 
     def late_sends(which, g, src, dst):
         here = pl.ds(SLOTS * g, SLOTS)
@@ -208,7 +221,7 @@
                 rx[here, :] = jnp.concatenate(
                     [rows[here, 128 * u + first : 128 * u + first + 64] for u in order], axis=1
                 )
-        early_x += early_sends(0, g, rx.at[here], rx)
+        x_copies.append(early_sends(0, g, rx.at[here], rx, (1, 3)))
 
         if g == 0:
             for copy in weights[0:4]:
@@ -235,7 +248,7 @@
             grad_copies.append(dispatch(1, 1, grads_in, raw))
         gout[here, :] = (weight[here, 0:1] * raw[here, :].astype(F32)).astype(BF)
         rg[here, :] = gout[here, mine]
-        early_g += early_sends(1, g, rg.at[here], rg)
+        g_copies.append(early_sends(1, g, rg.at[here], rg, (2, 1, 3) if g else (1, 3)))
         if g == 0:
             for copy in weights[4:6]:
                 copy.wait()
@@ -246,6 +259,17 @@
             columns = slice(QUARTER * j, QUARTER * (j + 1))
             gq[j, here, :] = jnp.concatenate([gup[here, columns], blank, ggp[here, columns], blank], axis=1)
         late_gu += late_sends(1, g, gq, rgu)
+
+    early_g = early_forward(1, 0, g_copies[0], rg) + g_copies[1]
+    early_x = early_forward(0, 0, x_copies[0], rx) + early_forward(0, 1, x_copies[1], rx)
+
+    slot_grad = dot(ggp[0:SLOTS, :], wg[...], NT) + dot(gup[0:SLOTS, :], wu[...], NT)
+    slot_send[...] = slot_grad.astype(BF)
+    returns = [
+        send(slot_send.at[block(n)], back.at[block(n)], ret_s.at[n], ret_r.at[n], (dp, (me + 4 - n) % 4))
+        for n in (2, 1, 3)
+    ]
+    back[0:MOST, :] = slot_send[0:MOST, :]
 
     chunk = half // 4
     rows_d = QPAD // 4
@@ -303,14 +327,6 @@
         sums.append(near_sends(part, part_gu.at[part - 1, 1], part_gu.at[part - 1, 3], got_gu.at[part - 1]))
     tile_gu(1, 0)
     tile_gu(2, 0)
-
-    slot_grad = dot(ggp[0:SLOTS, :], wg[...], NT) + dot(gup[0:SLOTS, :], wu[...], NT)
-    slot_send[...] = slot_grad.astype(BF)
-    returns = [
-        send(slot_send.at[block(n)], back.at[block(n)], ret_s.at[n], ret_r.at[n], (dp, (me + 4 - n) % 4))
-        for n in (2, 1, 3)
-    ]
-    back[0:MOST, :] = slot_send[0:MOST, :]
 
     scale = 1.0 / 32
     for copy in sums[0]:
@@ -408,7 +424,12 @@
 
 def store_kernel(*refs):
     sources, results, sems = refs[0:4], refs[4:8], refs[8]
-    copies = [pltpu.make_async_copy(sources[n], results[n], sems.at[n]) for n in range(4)]
+    pieces = 4
+    size = sources[0].shape[0] // pieces
+    copies = [pltpu.make_async_copy(sources[n], results[n], sems.at[n]) for n in range(1, 4)]
+    for k in range(pieces):
+        part = pl.ds(size * k, size)
+        copies.append(pltpu.make_async_copy(sources[0].at[part], results[0].at[part], sems.at[4 + k]))
     for copy in copies:
         copy.start()
     for copy in copies:
@@ -422,7 +443,7 @@
         out_shape=tuple(jax.ShapeDtypeStruct(value.shape, value.dtype) for value in results),
         in_specs=[pl.BlockSpec(memory_space=pltpu.VMEM)] * 4,
         out_specs=(pl.BlockSpec(memory_space=pl.ANY),) * 4,
-        scratch_shapes=[pltpu.SemaphoreType.DMA((4,))],
+        scratch_shapes=[pltpu.SemaphoreType.DMA((8,))],
         compiler_params=pltpu.CompilerParams(vmem_limit_bytes=4 * 2**20),
     )(*results)
 

time: 53.9 us -> 53.3 us (0.989)
  no operation moved by 1% of the time
where the time goes in v5:
time: 53.3 us; the launch traced here: 53.1 us
  Pallas kernels  52.3 us (98%)
  between operations  0.8 us (2%)
    pallas_call x1, Pallas kernels, main_pass(): pl.pallas_call(main_kernel, out_shape=(pltpu.VMEM(tokens.shape, BF), pltp...  50.7 us
    pallas_call x1, Pallas kernels, local(): pl.pallas_call(store_kernel, out_shape=tuple((jax.ShapeDtypeStruct(value....  1.57 us

profile of v5, /device:TPU:0, one launch (start us, length us, event | category | flops | bytes accessed | tf_op | source)
XLA Modules:
  0.0 53.1 jit_solution(641306132994001845)
XLA Ops:
  0.6 50.7 %shard_map.102 = (bf16[512,2048]{1,0:T(8,128)(2,1)S(1)}, bf16[1,64,1408]{2,1,0:T(8,128)(2,1)S(1)}, bf16[1,64,1408]{2,1,0:T(8,128)(2,1)S(1)}, bf16[1,44,2048]{2,1,0:T(8,128)(2,1)S(1)}) custom-call(s32[4,1024]{1,0:T(4,128)} %chosen_in.1, f32[1,1024]{1,0:T(1,128)} %slot_weight_in.1, bf16[512,2048]{1,0:T(8,128)(2,1)} %tokens.1, bf16[512,2048]{1,0:T(8,128)(2,1)} %out_grad.1, ...), custom_call_target="tpu_custom_call" | custom-call | tf_op jit(solution)/shard_map/pallas_call | solution.py:384
  51.4 1.6 %shard_map.103 = (bf16[512,2048]{1,0:T(8,128)(2,1)}, bf16[1,64,1408]{2,1,0:T(8,128)(2,1)}, bf16[1,64,1408]{2,1,0:T(8,128)(2,1)}, bf16[1,44,2048]{2,1,0:T(8,128)(2,1)}) custom-call(bf16[512,2048]{1,0:T(8,128)(2,1)S(1)} %get-tuple-element.8.refs_0_, bf16[1,64,1408]{2,1,0:T(8,128)(2,1)S(1)} %get-tuple-element.9.refs_1_, ...), custom_call_target="tpu_custom_call" | custom-call | tf_op jit(solution)/shard_map/pallas_call | solution.py:441

commit v6 on v5

--- a/solution.py
+++ b/solution.py
@@ -211,8 +211,6 @@
         here = pl.ds(SLOTS * g, SLOTS)
         for copy in row_copies[g]:
             copy.wait_recv()
-        if g == 0:
-            row_copies.append(dispatch(0, 1, rows_in, rows))
         for which in range(4):
             @pl.when(2 * core + yl == which)
             def _():
@@ -221,7 +219,9 @@
                 rx[here, :] = jnp.concatenate(
                     [rows[here, 128 * u + first : 128 * u + first + 64] for u in order], axis=1
                 )
-        x_copies.append(early_sends(0, g, rx.at[here], rx, (1, 3)))
+        x_copies.append(early_sends(0, g, rx.at[here], rx, (1, 3) if g else (2, 1, 3)))
+        if g == 0:
+            row_copies.append(dispatch(0, 1, rows_in, rows))
 
         if g == 0:
             for copy in weights[0:4]:
@@ -244,11 +244,11 @@
 
         for copy in grad_copies[g]:
             copy.wait_recv()
-        if g == 0:
-            grad_copies.append(dispatch(1, 1, grads_in, raw))
         gout[here, :] = (weight[here, 0:1] * raw[here, :].astype(F32)).astype(BF)
         rg[here, :] = gout[here, mine]
         g_copies.append(early_sends(1, g, rg.at[here], rg, (2, 1, 3) if g else (1, 3)))
+        if g == 0:
+            grad_copies.append(dispatch(1, 1, grads_in, raw))
         if g == 0:
             for copy in weights[4:6]:
                 copy.wait()
@@ -261,7 +261,7 @@
         late_gu += late_sends(1, g, gq, rgu)
 
     early_g = early_forward(1, 0, g_copies[0], rg) + g_copies[1]
-    early_x = early_forward(0, 0, x_copies[0], rx) + early_forward(0, 1, x_copies[1], rx)
+    early_x = x_copies[0] + early_forward(0, 1, x_copies[1], rx)
 
     slot_grad = dot(ggp[0:SLOTS, :], wg[...], NT) + dot(gup[0:SLOTS, :], wu[...], NT)
     slot_send[...] = slot_grad.astype(BF)

time: 53.3 us -> 53 us (level)
  no operation moved by 1% of the time
where the time goes in v6:
time: 53 us; the launch traced here: 52.8 us
  Pallas kernels  52 us (98%)
  between operations  0.8 us (2%)
    pallas_call x1, Pallas kernels, main_pass(): pl.pallas_call(main_kernel, out_shape=(pltpu.VMEM(tokens.shape, BF), pltp...  50.4 us
    pallas_call x1, Pallas kernels, local(): pl.pallas_call(store_kernel, out_shape=tuple((jax.ShapeDtypeStruct(value....  1.57 us

profile of v6, /device:TPU:0, one launch (start us, length us, event | category | flops | bytes accessed | tf_op | source)
XLA Modules:
  0.0 52.8 jit_solution(8143661793039383422)
XLA Ops:
  0.6 50.4 %shard_map.102 = (bf16[512,2048]{1,0:T(8,128)(2,1)S(1)}, bf16[1,64,1408]{2,1,0:T(8,128)(2,1)S(1)}, bf16[1,64,1408]{2,1,0:T(8,128)(2,1)S(1)}, bf16[1,44,2048]{2,1,0:T(8,128)(2,1)S(1)}) custom-call(s32[4,1024]{1,0:T(4,128)} %chosen_in.1, f32[1,1024]{1,0:T(1,128)} %slot_weight_in.1, bf16[512,2048]{1,0:T(8,128)(2,1)} %tokens.1, bf16[512,2048]{1,0:T(8,128)(2,1)} %out_grad.1, ...), custom_call_target="tpu_custom_call" | custom-call | tf_op jit(solution)/shard_map/pallas_call | solution.py:384
  51.1 1.6 %shard_map.103 = (bf16[512,2048]{1,0:T(8,128)(2,1)}, bf16[1,64,1408]{2,1,0:T(8,128)(2,1)}, bf16[1,64,1408]{2,1,0:T(8,128)(2,1)}, bf16[1,44,2048]{2,1,0:T(8,128)(2,1)}) custom-call(bf16[512,2048]{1,0:T(8,128)(2,1)S(1)} %get-tuple-element.8.refs_0_, bf16[1,64,1408]{2,1,0:T(8,128)(2,1)S(1)} %get-tuple-element.9.refs_1_, ...), custom_call_target="tpu_custom_call" | custom-call | tf_op jit(solution)/shard_map/pallas_call | solution.py:441
